TPU v7x, 256 devices: a whole 4x4x8 slice. The times are simulated.
256 devices in a mesh: dp: 4 (over y), seq: 64 (over z, x, core).
Axes of the slice: x: 4, y: 4, z: 8, core: 2. Of those that a mesh axis runs over, the one named last changes fastest.
Arguments:
- queries: bfloat16 [4, 8192, 8192], P('dp', 'seq'), may hold values from -6 to 6
- keys: bfloat16 [4, 8192, 1024], P('dp', 'seq'), may hold values from -6 to 6
- values: bfloat16 [4, 8192, 1024], P('dp', 'seq'), may hold values from -6 to 6
- grad_out: bfloat16 [4, 8192, 8192], P('dp', 'seq'), may hold values from -6 to 6
- q_gain: float32 [64, 128], P('seq'), may hold values from 0.1 to 1.9
- k_gain: float32 [8, 128], replicated, may hold values from 0.1 to 1.9
- block_lists: int32 [4, 128, 8], P('dp'), may hold values from 0 to 127, as said below
Outputs:
- attended: bfloat16 [4, 8192, 8192], P('dp', 'seq')
- grad_queries: bfloat16 [4, 8192, 8192], P('dp', 'seq')
- grad_keys: bfloat16 [4, 8192, 1024], P('dp', 'seq')
- grad_values: bfloat16 [4, 8192, 1024], P('dp', 'seq')
- grad_q_gain: float32 [64, 128], P('seq')
- grad_k_gain: float32 [8, 128], replicated
Inputs may be any that keep to these rules, and one draw needn't show every extreme that they name: `block_lists`: for query block i, slots 0 to 2 hold blocks i - 1 + s modulo 128, the next 2 slots hold blocks 0 to 1, the last 3 any blocks; entries may repeat.
All inputs are finite; a program needn't handle non-finite values.
Results may differ from a plain program's by a relative error of at most 0.0085.
Values may be sent and summed in bfloat16 or wider, within the bound.
A program may use at most 192 MiB of HBM per device.

v0:
```python
import math

import jax
import jax.numpy as jnp
import numpy as np
from jax import lax
from jax.sharding import PartitionSpec as P

EPSILON = 1e-06


def on_device(queries, keys, values, grad_out, q_gain, k_gain, block_lists):
    seq_width = lax.axis_size("seq")
    tok_count = queries.shape[1]
    head_size = q_gain.shape[1]
    heads_here = q_gain.shape[0]
    heads_all = heads_here * seq_width
    kv_all = k_gain.shape[0]
    group_size = heads_all // kv_all
    kv_here = max(1, heads_here // group_size)
    repeat_count = heads_here // kv_here
    slot_dev = np.arange(seq_width * kv_here) // kv_here
    slot_part = np.arange(seq_width * kv_here) % kv_here
    kv_order = (slot_dev * heads_here // group_size + slot_part).astype(np.int32)
    query_send = queries.reshape(tok_count, heads_all, head_size)
    grad_send = grad_out.reshape(tok_count, heads_all, head_size)
    key_send = jnp.take(keys.reshape(tok_count, kv_all, head_size), kv_order, axis=1)
    value_send = jnp.take(values.reshape(tok_count, kv_all, head_size), kv_order, axis=1)
    query_heads, key_heads, value_heads, grad_heads = (
        lax.all_to_all(query_send, "seq", split_axis=1, concat_axis=0, tiled=True),
        lax.all_to_all(key_send, "seq", split_axis=1, concat_axis=0, tiled=True),
        lax.all_to_all(value_send, "seq", split_axis=1, concat_axis=0, tiled=True),
        lax.all_to_all(grad_send, "seq", split_axis=1, concat_axis=0, tiled=True),
    )
    seq_len = query_heads.shape[0]
    kv_base = lax.axis_index("seq") * heads_here // group_size
    gain_k = lax.dynamic_slice_in_dim(k_gain, kv_base, kv_here, 0)
    query_float = query_heads.astype(jnp.float32)
    query_scale = lax.rsqrt(jnp.mean(query_float * query_float, -1, keepdims=True) + EPSILON)
    query_normed = (query_float * query_scale * q_gain).astype(jnp.bfloat16)
    key_float = key_heads.astype(jnp.float32)
    key_scale = lax.rsqrt(jnp.mean(key_float * key_float, -1, keepdims=True) + EPSILON)
    key_normed = (key_float * key_scale * gain_k).astype(jnp.bfloat16)
    key_wide = jnp.repeat(key_normed, repeat_count, axis=1)
    value_wide = jnp.repeat(value_heads, repeat_count, axis=1)
    lists = block_lists[0]
    block_count = lists.shape[0]
    block_len = seq_len // block_count
    per_step = math.gcd(block_count, max(1, 512 // block_len))
    step_count = block_count // per_step
    score_scale = 1.0 / math.sqrt(head_size)
    query_tiles = query_normed.reshape(block_count, block_len, heads_here, head_size)
    key_tiles = key_wide.reshape(block_count, block_len, heads_here, head_size)
    value_tiles = value_wide.reshape(block_count, block_len, heads_here, head_size)
    grad_tiles = grad_heads.reshape(block_count, block_len, heads_here, head_size)

    def block_inputs(step_id):
        listed = lax.dynamic_slice_in_dim(lists, step_id * per_step, per_step, 0)
        query_block = lax.dynamic_slice_in_dim(query_tiles, step_id * per_step, per_step, 0)
        return (listed, query_block, key_tiles[listed], value_tiles[listed])

    def make_probs(query_block, key_block):
        scores = (
            jnp.einsum(
                "nihd,nkjhd->nhikj", query_block, key_block, preferred_element_type=jnp.float32
            )
            * score_scale
        )
        expo = jnp.exp(scores)
        return expo / jnp.sum(expo, axis=(3, 4), keepdims=True)

    def attend(probs, value_block):
        return jnp.einsum(
            "nhikj,nkjhd->nihd",
            probs.astype(jnp.bfloat16),
            value_block,
            preferred_element_type=jnp.float32,
        ).astype(jnp.bfloat16)

    def backward_core(carry, step_id, listed, query_block, key_block, value_block, probs):
        key_total, value_total = carry
        grad_block = lax.dynamic_slice_in_dim(grad_tiles, step_id * per_step, per_step, 0)
        probs_low = probs.astype(jnp.bfloat16)
        dprobs = jnp.einsum(
            "nihd,nkjhd->nhikj", grad_block, value_block, preferred_element_type=jnp.float32
        )
        delta = jnp.sum(probs * dprobs, axis=(3, 4), keepdims=True)
        dscores = (probs * (dprobs - delta)).astype(jnp.bfloat16)
        dq_block = (
            jnp.einsum("nhikj,nkjhd->nihd", dscores, key_block, preferred_element_type=jnp.float32)
            * score_scale
        )
        key_terms = (
            jnp.einsum(
                "nhikj,nihd->nkjhd", dscores, query_block, preferred_element_type=jnp.float32
            )
            * score_scale
        )
        value_terms = jnp.einsum(
            "nhikj,nihd->nkjhd", probs_low, grad_block, preferred_element_type=jnp.float32
        )
        return (
            (key_total.at[listed].add(key_terms), value_total.at[listed].add(value_terms)),
            dq_block,
        )

    empty_total = jnp.zeros((block_count, block_len, heads_here, head_size), jnp.float32)
    steps_all = jnp.arange(step_count)

    def late_step(carry, step_id):
        listed, query_block, key_block, value_block = block_inputs(step_id)
        probs = make_probs(query_block, key_block)
        attended_block = attend(probs, value_block)
        carry, dq_block = backward_core(
            carry, step_id, listed, query_block, key_block, value_block, probs
        )
        return (carry, (dq_block, attended_block))

    (dk_normed, dv_total), (dq_blocks, attended_blocks) = lax.scan(
        late_step, (empty_total, empty_total), steps_all
    )
    attended_heads = attended_blocks.reshape(seq_len, heads_here, head_size)
    dq_normed = dq_blocks.reshape(seq_len, heads_here, head_size)
    dk_normed = dk_normed.reshape(seq_len, heads_here, head_size)
    dv_head = dv_total.reshape(seq_len, heads_here, head_size).astype(jnp.bfloat16)
    grad_query = query_scale * (
        q_gain * dq_normed
        - query_float
        * query_scale
        * query_scale
        * jnp.mean(query_float * q_gain * dq_normed, -1, keepdims=True)
    )
    grad_query = grad_query.astype(jnp.bfloat16)
    key_float_wide = jnp.repeat(key_float, repeat_count, axis=1)
    key_scale_wide = jnp.repeat(key_scale, repeat_count, axis=1)
    gain_k_wide = jnp.repeat(gain_k, repeat_count, axis=0)
    dk_head = key_scale_wide * (
        gain_k_wide * dk_normed
        - key_float_wide
        * key_scale_wide
        * key_scale_wide
        * jnp.mean(key_float_wide * gain_k_wide * dk_normed, -1, keepdims=True)
    )
    dk_head = dk_head.astype(jnp.bfloat16)
    gain_q_part = jnp.sum(dq_normed * query_float * query_scale, 0)
    gain_k_part = jnp.sum(
        jnp.sum(dk_normed * key_float_wide * key_scale_wide, 0).reshape(
            kv_here, repeat_count, head_size
        ),
        1,
    )
    attended_local, dq_local, dk_local, dv_local = (
        lax.all_to_all(attended_heads, "seq", split_axis=0, concat_axis=1, tiled=True),
        lax.all_to_all(grad_query, "seq", split_axis=0, concat_axis=1, tiled=True),
        lax.all_to_all(dk_head, "seq", split_axis=0, concat_axis=1, tiled=True),
        lax.all_to_all(dv_head, "seq", split_axis=0, concat_axis=1, tiled=True),
    )
    dk_sum = jnp.sum(
        dk_local.astype(jnp.float32).reshape(tok_count, kv_all, group_size, head_size), 2
    )
    dv_sum = jnp.sum(
        dv_local.astype(jnp.float32).reshape(tok_count, kv_all, group_size, head_size), 2
    )
    key_rows = lax.dynamic_update_slice(
        jnp.zeros((kv_all, head_size), jnp.float32), gain_k_part, (kv_base, 0)
    )
    gain_q_grad = lax.psum(gain_q_part, "dp")
    gain_k_grad = lax.psum(key_rows, ("dp", "seq"))
    return (
        attended_local.reshape(1, tok_count, heads_all * head_size),
        dq_local.reshape(1, tok_count, heads_all * head_size),
        dk_sum.astype(jnp.bfloat16).reshape(1, tok_count, kv_all * head_size),
        dv_sum.astype(jnp.bfloat16).reshape(1, tok_count, kv_all * head_size),
        gain_q_grad,
        gain_k_grad,
    )


def solution(mesh):
    return jax.shard_map(
        on_device,
        mesh=mesh,
        in_specs=(
            P("dp", "seq", None),
            P("dp", "seq", None),
            P("dp", "seq", None),
            P("dp", "seq", None),
            P("seq", None),
            P(),
            P("dp", None, None),
        ),
        out_specs=(
            P("dp", "seq", None),
            P("dp", "seq", None),
            P("dp", "seq", None),
            P("dp", "seq", None),
            P("seq", None),
            P(),
        ),
        check_vma=False,
    )
```

profile of v0, /device:TPU:1, one launch (start us, length us, event | category | flops | bytes accessed | tf_op | source)
XLA Modules:
  0.0 1169.7 jit_solution(5436756964261432090)
XLA Ops:
  4.8 13.0 %all-to-all-start.1 = ((bf16[128,64,128]{2,0,1:T(8,128)(2,1)}), bf16[128,64,128]{2,0,1:T(8,128)(2,1)S(1)}, u32[]{:S(2)}, u32[]{:S(2)}) async-start(bf16[128,64,128]{2,0,1:T(8,128)(2,1)} %bitcast.289), calls=%async_computation.1 | async-start | bytes 4194304 | tf_op jit(solution)/shard_map/all_to_all | solution.py:31
  22.6 44.8 %all-to-all-done.1 = bf16[128,64,128]{2,0,1:T(8,128)(2,1)S(1)} async-done(((bf16[128,64,128]{2,0,1:T(8,128)(2,1)}), bf16[128,64,128]{2,0,1:T(8,128)(2,1)S(1)}, u32[]{:S(2)}, u32[]{:S(2)}) %all-to-all-start.1) | async-done | bytes 2097184 | tf_op jit(solution)/shard_map/all_to_all | solution.py:31
  77.2 47.1 %all-to-all-done = bf16[128,64,128]{2,0,1:T(8,128)(2,1)} async-done(((bf16[128,64,128]{2,0,1:T(8,128)(2,1)}), bf16[128,64,128]{2,0,1:T(8,128)(2,1)}, u32[]{:S(2)}, u32[]{:S(2)}) %all-to-all-start) | async-done | bytes 2097184 | tf_op jit(solution)/shard_map/all_to_all | solution.py:30
  136.2 44.8 %all-to-all-done.3 = bf16[128,64,128]{2,0,1:T(8,128)(2,1)S(1)} async-done(((bf16[128,64,128]{2,0,1:T(8,128)(2,1)}), bf16[128,64,128]{2,0,1:T(8,128)(2,1)S(1)}, u32[]{:S(2)}, u32[]{:S(2)}) %all-to-all-start.3) | async-done | bytes 2097184 | tf_op jit(solution)/shard_map/all_to_all | solution.py:32
  207.0 32.6 %all-to-all-done.2 = bf16[128,64,128]{2,0,1:T(8,128)(2,1)} async-done(((bf16[128,64,128]{2,0,1:T(8,128)(2,1)}), bf16[128,64,128]{2,0,1:T(8,128)(2,1)}, u32[]{:S(2)}, u32[]{:S(2)}) %all-to-all-start.2) | async-done | bytes 2097184 | tf_op jit(solution)/shard_map/all_to_all | solution.py:33
  244.5 570.0 %while.16 = (s32[]{:T(128)}, f32[128,64,1,128]{3,1,0,2:T(8,128)}, f32[128,64,1,128]{3,1,0,2:T(8,128)}, f32[16,8,64,1,128]{4,2,1,3,0:T(8,128)}, bf16[16,8,64,1,12...) while((s32[]{:T(128)}, f32[128,64,1,128]{3,1,0,2:T(8,128)}, ...), condition=%wide.region_7.9_spmd, body=%wide.region_2.8_spmd.sunk | while | flops 407503040 | bytes 64898660 | solution.py:119
  256.7 9.1 scatter_fusion
  267.4 9.1 scatter_fusion.1
  292.3 9.0 scatter_fusion
  303.0 9.1 scatter_fusion.1
  363.5 9.0 scatter_fusion
  374.2 9.0 scatter_fusion.1
  434.7 9.1 scatter_fusion
  445.4 9.1 scatter_fusion.1
  470.5 9.1 scatter_fusion
  506.1 9.0 scatter_fusion
  516.8 9.1 scatter_fusion.1
  552.4 9.1 scatter_fusion.1
  577.4 9.1 scatter_fusion
  648.6 9.1 scatter_fusion
  684.2 9.1 scatter_fusion
  694.9 9.0 scatter_fusion.1
  766.1 9.0 scatter_fusion.1
  791.0 9.1 scatter_fusion
  862.5 28.4 %all-to-all-done.6 = bf16[64,2,8192]{2,1,0:T(2,128)(2,1)S(1)} async-done(((bf16[64,2,8192]{2,1,0:T(2,128)(2,1)}), bf16[64,2,8192]{2,1,0:T(2,128)(2,1)S(1)}, u32[]{:S(2)}, u32[]{:S(2)}) %all-to-all-start.6) | async-done | bytes 2097184 | tf_op jit(solution)/shard_map/all_to_all | solution.py:155
  906.6 41.1 %all-to-all-done.5 = bf16[64,2,8192]{2,1,0:T(2,128)(2,1)} async-done(((bf16[64,2,8192]{2,1,0:T(2,128)(2,1)}), bf16[64,2,8192]{2,1,0:T(2,128)(2,1)}, u32[]{:S(2)}, u32[]{:S(2)}) %all-to-all-start.5) | async-done | bytes 2097184 | tf_op jit(solution)/shard_map/all_to_all | solution.py:154
  967.4 37.1 %all-to-all-done.4 = bf16[64,2,8192]{2,1,0:T(2,128)(2,1)} async-done(((bf16[64,2,8192]{2,1,0:T(2,128)(2,1)}), bf16[64,2,8192]{2,1,0:T(2,128)(2,1)}, u32[]{:S(2)}, u32[]{:S(2)}) %all-to-all-start.4) | async-done | bytes 2097184 | tf_op jit(solution)/shard_map/all_to_all | solution.py:153
  1011.8 10.3 psum.14
  1022.1 82.6 %psum.15 = f32[8,128]{1,0:T(8,128)} all-reduce(f32[8,128]{1,0:T(8,128)S(1)} %dynamic_update_slice.11), channel_id=1, replica_groups=mesh['dp'=4,'seq'=64] {'dp','seq'}, use_global_device_ids=true, to_apply=%region_15.17 | all-reduce | flops 1024 | bytes 8192 | tf_op jit(solution)/shard_map/psum | solution.py:168
  1115.3 10.4 reshape.880
  1135.2 10.4 reshape.878
  1155.1 10.4 reshape.884
  (490 shorter events, 579.8 us)
Async XLA Ops:
  0.6 189.7 %copy-start = (f32[8,128]{1,0:T(8,128)S(1)}, f32[8,128]{1,0:T(8,128)}, u32[]{:S(2)}) copy-start(f32[8,128]{1,0:T(8,128)} %param.17) | copy-start | bytes 12292
  4.8 62.7 %all-to-all-start.1 = ((bf16[128,64,128]{2,0,1:T(8,128)(2,1)}), bf16[128,64,128]{2,0,1:T(8,128)(2,1)S(1)}, u32[]{:S(2)}, u32[]{:S(2)}) async-start(bf16[128,64,128]{2,0,1:T(8,128)(2,1)} %bitcast.289), calls=%async_computation.1 | async-start | bytes 4194304 | tf_op jit(solution)/shard_map/all_to_all | solution.py:31
  22.6 52.1 %copy-start.12 = (bf16[1,128,1024]{2,1,0:T(8,128)(2,1)S(1)}, bf16[1,128,1024]{2,1,0:T(8,128)(2,1)}, u32[]{:S(2)}) copy-start(bf16[1,128,1024]{2,1,0:T(8,128)(2,1)} %param.14) | copy-start | bytes 786436
  67.4 7.4 copy-start.10
  67.4 56.8 %all-to-all-start = ((bf16[128,64,128]{2,0,1:T(8,128)(2,1)}), bf16[128,64,128]{2,0,1:T(8,128)(2,1)}, u32[]{:S(2)}, u32[]{:S(2)}) async-start(bf16[128,64,128]{2,0,1:T(8,128)(2,1)} %copy.111), calls=%async_computation | async-start | bytes 4194304 | tf_op jit(solution)/shard_map/all_to_all | solution.py:30
  124.2 56.7 %all-to-all-start.3 = ((bf16[128,64,128]{2,0,1:T(8,128)(2,1)}), bf16[128,64,128]{2,0,1:T(8,128)(2,1)S(1)}, u32[]{:S(2)}, u32[]{:S(2)}) async-start(bf16[128,64,128]{2,0,1:T(8,128)(2,1)} %bitcast.288), calls=%async_computation.3 | async-start | bytes 4194304 | tf_op jit(solution)/shard_map/all_to_all | solution.py:32
  136.2 54.0 %copy-start.14 = (s32[1,128,8]{1,2,0:T(8,128)S(1)}, s32[1,128,8]{1,2,0:T(8,128)}, u32[]{:S(2)}) copy-start(s32[1,128,8]{1,2,0:T(8,128)} %param.18) | copy-start | bytes 12292
  182.3 57.2 %all-to-all-start.2 = ((bf16[128,64,128]{2,0,1:T(8,128)(2,1)}), bf16[128,64,128]{2,0,1:T(8,128)(2,1)}, u32[]{:S(2)}, u32[]{:S(2)}) async-start(bf16[128,64,128]{2,0,1:T(8,128)(2,1)} %copy.114), calls=%async_computation.2 | async-start | bytes 4194304 | tf_op jit(solution)/shard_map/all_to_all | solution.py:33
  190.3 5.9 copy-start.11
  196.7 3.7 copy-start.6
  196.7 5.6 copy-start.13
  276.4 3.7 copy-start.8
  312.1 3.7 copy-start.8
  347.6 3.7 copy-start.8
  383.2 3.7 copy-start.8
  418.8 3.7 copy-start.8
  454.6 3.7 copy-start.8
  490.2 3.7 copy-start.8
  525.9 3.7 copy-start.8
  561.5 3.7 copy-start.8
  597.2 3.7 copy-start.8
  632.7 3.7 copy-start.8
  668.3 3.7 copy-start.8
  704.0 3.7 copy-start.8
  739.6 3.7 copy-start.8
  775.1 3.7 copy-start.8
  810.8 3.7 copy-start.8
  834.1 56.8 %all-to-all-start.6 = ((bf16[64,2,8192]{2,1,0:T(2,128)(2,1)}), bf16[64,2,8192]{2,1,0:T(2,128)(2,1)S(1)}, u32[]{:S(2)}, u32[]{:S(2)}) async-start(bf16[64,2,8192]{2,1,0:T(2,128)(2,1)} %reshape.881), calls=%async_computation.6 | async-start | bytes 4194304 | tf_op jit(solution)/shard_map/all_to_all | solution.py:155
  890.9 56.8 %all-to-all-start.5 = ((bf16[64,2,8192]{2,1,0:T(2,128)(2,1)}), bf16[64,2,8192]{2,1,0:T(2,128)(2,1)}, u32[]{:S(2)}, u32[]{:S(2)}) async-start(bf16[64,2,8192]{2,1,0:T(2,128)(2,1)} %reshape.879), calls=%async_computation.5 | async-start | bytes 4194304 | tf_op jit(solution)/shard_map/all_to_all | solution.py:154
  947.7 56.8 %all-to-all-start.4 = ((bf16[64,2,8192]{2,1,0:T(2,128)(2,1)}), bf16[64,2,8192]{2,1,0:T(2,128)(2,1)}, u32[]{:S(2)}, u32[]{:S(2)}) async-start(bf16[64,2,8192]{2,1,0:T(2,128)(2,1)} %reshape.877), calls=%async_computation.4 | async-start | bytes 4194304 | tf_op jit(solution)/shard_map/all_to_all | solution.py:153
  1004.5 150.6 %all-to-all-start.7 = ((bf16[64,2,8192]{2,1,0:T(2,128)(2,1)}), bf16[64,2,8192]{2,1,0:T(2,128)(2,1)}, u32[]{:S(2)}, u32[]{:S(2)}) async-start(bf16[64,2,8192]{2,1,0:T(2,128)(2,1)} %reshape.883), calls=%async_computation.7 | async-start | bytes 4194304 | tf_op jit(solution)/shard_map/all_to_all | solution.py:156
  1165.6 3.9 copy-start.1
  (66 other events, 149.1 us)
where the time goes:
time: 1190 us; the launch traced here: 1170 us
  other arithmetic  382 us (32%)
  waiting for transfers between devices  276 us (23%)
  local copies, waits for them, and re-layouts  179 us (15%)
  matrix products  162 us (14%)
  blocking collectives  92.9 us (8%)
  starting transfers between devices  63.8 us (5%)
  loops' own time  12.3 us (1%)
    scatter-add x16, other arithmetic, backward_core(): value_total.at[listed].add(value_terms)  145 us
    scatter-add x16, other arithmetic, backward_core(): key_total.at[listed].add(key_terms)  145 us
    psum x1, blocking collectives, on_device(): gain_k_grad = lax.psum(key_rows, ('dp', 'seq'))  82.6 us
    unnamed x41, local copies, waits for them, and re-layouts  80.8 us
    gather x32, local copies, waits for them, and re-layouts, block_inputs(): return (listed, query_block, key_tiles[listed], value_tiles[listed])  64 us
    while x32, matrix products  49 us
    all_to_all x1, waiting for transfers between devices, on_device(): lax.all_to_all(query_send, 'seq', split_axis=1, concat_axis=0, tiled=True)  47.1 us
    all_to_all x1, waiting for transfers between devices, on_device(): lax.all_to_all(key_send, 'seq', split_axis=1, concat_axis=0, tiled=True)  44.8 us
  transfers between devices with their start and end apart: 8, of which 7 were waited for; matrix products, arithmetic and copies ran while one was open for 10% of the time, Pallas kernels for 0%

commit v1 on v0

v1 whole, which is shorter than its diff:
```python
import functools
import math

import jax
import jax.numpy as jnp
from jax import lax
from jax.experimental import pallas as pl
from jax.experimental.pallas import tpu as pltpu
from jax.sharding import PartitionSpec as P

EPSILON = 1e-06
BLOCK = 64
SUBS = 2
MESH = pl.DeviceIdType.MESH
ANY = pl.BlockSpec(memory_space=pl.ANY)
VMEM = pl.BlockSpec(memory_space=pltpu.VMEM)
LIMIT = 56 * 1024 * 1024


def place(cols):
    seq = lax.axis_index("seq")
    return lax.axis_index("dp"), seq // cols, seq % cols


def greet(devices):
    barrier = pltpu.get_barrier_semaphore()
    for device in devices:
        pl.semaphore_signal(barrier, inc=1, device_id=device, device_id_type=MESH)
    pl.semaphore_wait(barrier, len(devices))


def push(src, dst, send_sem, recv_sem, device):
    copy = pltpu.make_async_remote_copy(
        src_ref=src,
        dst_ref=dst,
        send_sem=send_sem,
        recv_sem=recv_sem,
        device_id=device,
        device_id_type=MESH,
    )
    copy.start()
    return copy


def move(src, dst, sem):
    copy = pltpu.make_async_copy(src, dst, sem)
    copy.start()
    return copy


def aligned(index, size):
    return pl.ds(pl.multiple_of(index * size, size), size)


def gather_kernel(
    rows,
    cols,
    q_ref,
    go_ref,
    k_ref,
    v_ref,
    qg_ref,
    kg_ref,
    qh_ref,
    goh_ref,
    kall_ref,
    vall_ref,
    gq_ref,
    kx,
    vx,
    kn,
    gain,
    gx,
    gz,
    own_sem,
    wide_send,
    wide_recv,
    kv_send,
    kv_recv,
    gx_send,
    gx_recv,
    k_send,
    k_recv,
    v_send,
    v_recv,
    gz_send,
    gz_recv,
):
    dp, z, c = place(cols)
    tok = q_ref.shape[0]
    width = q_ref.shape[1] // cols
    head = k_ref.shape[1] // cols

    def at(zz, cc):
        return (dp, lax.rem(zz, rows) * cols + lax.rem(cc, cols))

    right, left = at(z + 1, c), at(z + rows - 1, c)
    partners = {d: at(z, c + d) for d in range(1, cols)}
    gain[...] = jnp.broadcast_to(qg_ref[...], gain.shape)
    greet(list(partners.values()) + [right, left])

    mine = aligned(c, tok)
    small, large, local = [], [], []
    for d in range(1, cols):
        part = aligned(lax.rem(c + d, cols), head)
        for i, (src, dst) in enumerate(((k_ref, kx), (v_ref, vx))):
            small.append(
                push(src.at[:, part], dst.at[mine, :], kv_send.at[i, d], kv_recv.at[i, d], partners[d])
            )
        small.append(push(gain, gx.at[c], gx_send.at[d], gx_recv.at[d], partners[d]))
    own = [
        move(src.at[:, aligned(c, head)], dst.at[mine, :], own_sem.at[i])
        for i, (src, dst) in enumerate(((k_ref, kx), (v_ref, vx)))
    ]
    for d in range(1, cols):
        part = aligned(lax.rem(c + d, cols), width)
        for i, (src, dst) in enumerate(((q_ref, qh_ref), (go_ref, goh_ref))):
            large.append(
                push(src.at[:, part], dst.at[mine, :], wide_send.at[i, d], wide_recv.at[i, d], partners[d])
            )
    for i, (src, dst) in enumerate(((q_ref, qh_ref), (go_ref, goh_ref))):
        local.append(move(src.at[:, aligned(c, width)], dst.at[mine, :], own_sem.at[2 + i]))

    for copy in own + small:
        copy.wait()
    key = kx[...].astype(jnp.float32)
    scale = lax.rsqrt(jnp.mean(key * key, -1, keepdims=True) + EPSILON)
    kn[...] = (key * scale * kg_ref[pl.ds(c, 1), :]).astype(jnp.bfloat16)
    gx[c] = gain[...]
    gz[z] = jnp.concatenate([gx[i, :1, :] for i in range(cols)], axis=0)
    local.append(move(kn, kall_ref.at[z], own_sem.at[4]))
    local.append(move(vx, vall_ref.at[z], own_sem.at[5]))

    sub = kn.shape[0] // SUBS
    ring = {}
    for t in range(rows - 1):
        k_slot, v_slot = lax.rem(z + rows - t, rows), lax.rem(z + t, rows)
        for s in range(SUBS):
            part = pl.ds(s * sub, sub)
            k_dst, v_dst = kall_ref.at[k_slot, part, :], vall_ref.at[v_slot, part, :]
            if t:
                ring["k", t - 1, s].wait_recv()
            k_src = k_dst if t else kn.at[part, :]
            ring["k", t, s] = push(k_src, k_dst, k_send.at[t, s], k_recv.at[t, s], right)
            if t:
                ring["v", t - 1, s].wait_recv()
            v_src = v_dst if t else vx.at[part, :]
            ring["v", t, s] = push(v_src, v_dst, v_send.at[t, s], v_recv.at[t, s], left)
        if t:
            ring["g", t - 1, 0].wait_recv()
        ring["g", t, 0] = push(gz.at[k_slot], gz.at[k_slot], gz_send.at[t], gz_recv.at[t], right)
    for (_, t, _), copy in ring.items():
        if t == rows - 2:
            copy.wait_recv()
        copy.wait_send()
    gq_ref[...] = gz[c]
    for copy in local + large:
        copy.wait()


def gather(rows, cols, queries, grad_out, keys, values, q_gain, k_gain):
    tok, wide = queries.shape
    head = keys.shape[1] // cols
    group = cols * tok
    sem = pltpu.SemaphoreType.DMA
    low = jnp.bfloat16
    return pl.pallas_call(
        functools.partial(gather_kernel, rows, cols),
        out_shape=(
            jax.ShapeDtypeStruct((group, wide // cols), low),
            jax.ShapeDtypeStruct((group, wide // cols), low),
            jax.ShapeDtypeStruct((rows, group, head), low),
            jax.ShapeDtypeStruct((rows, group, head), low),
            jax.ShapeDtypeStruct((cols, head), jnp.float32),
        ),
        in_specs=[ANY] * 4 + [VMEM] * 2,
        out_specs=(ANY, ANY, ANY, ANY, VMEM),
        scratch_shapes=[
            pltpu.VMEM((group, head), low),
            pltpu.VMEM((group, head), low),
            pltpu.VMEM((group, head), low),
            pltpu.VMEM((8, head), jnp.float32),
            pltpu.VMEM((cols, 8, head), jnp.float32),
            pltpu.VMEM((rows, cols, head), jnp.float32),
            sem((6,)),
            sem((2, cols)),
            sem((2, cols)),
            sem((2, cols)),
            sem((2, cols)),
            sem((cols,)),
            sem((cols,)),
            sem((rows, SUBS)),
            sem((rows, SUBS)),
            sem((rows, SUBS)),
            sem((rows, SUBS)),
            sem((rows,)),
            sem((rows,)),
        ],
        compiler_params=pltpu.CompilerParams(
            collective_id=0, has_side_effects=True, vmem_limit_bytes=LIMIT
        ),
        cost_estimate=pl.CostEstimate(flops=0, bytes_accessed=16 << 20, transcendentals=0),
    )(queries, grad_out, keys, values, q_gain, k_gain)


def dot(a, b, dims):
    return lax.dot_general(a, b, (dims, ((), ())), preferred_element_type=jnp.float32)


def attend_kernel(
    cols,
    steps,
    slots,
    lists_ref,
    q_ref,
    go_ref,
    k_ref,
    v_ref,
    gq_ref,
    kg_ref,
    a_ref,
    dq_ref,
    dk_ref,
    dv_ref,
    gp_ref,
    dk_acc,
    dv_acc,
    gq_acc,
):
    n = pl.program_id(0)
    _, z, c = place(cols)
    head = k_ref.shape[1]
    heads = q_ref.shape[1] // head
    score_scale = 1.0 / math.sqrt(head)

    @pl.when(n == 0)
    def _():
        dk_acc[...] = jnp.zeros_like(dk_acc)
        dv_acc[...] = jnp.zeros_like(dv_acc)
        gq_acc[...] = jnp.zeros_like(gq_acc)

    ids = [lists_ref[(z * steps + n) * slots + s] for s in range(slots)]
    spans = [aligned(i, BLOCK) for i in ids]
    key = jnp.concatenate([k_ref[span, :] for span in spans], axis=0)
    value = jnp.concatenate([v_ref[span, :] for span in spans], axis=0)
    cut = [slice(h * head, (h + 1) * head) for h in range(heads)]
    raw = [q_ref[:, s].astype(jnp.float32) for s in cut]
    scales = [lax.rsqrt(jnp.mean(x * x, -1, keepdims=True) + EPSILON) for x in raw]
    normed = jnp.concatenate(
        [(x * s * gq_ref[h : h + 1, :]).astype(jnp.bfloat16) for h, (x, s) in enumerate(zip(raw, scales))],
        axis=0,
    )
    grad = jnp.concatenate([go_ref[:, s] for s in cut], axis=0)

    scores = dot(key, normed, ((1,), (1,)))
    expo = jnp.exp2(scores * (score_scale * math.log2(math.e)))
    probs = expo * (1.0 / jnp.sum(expo, axis=0, keepdims=True))
    low = probs.astype(jnp.bfloat16)
    out = dot(value, low, ((0,), (0,))).T
    dprobs = dot(value, grad, ((1,), (1,)))
    delta = jnp.sum(probs * dprobs, axis=0, keepdims=True)
    dscores = (probs * (dprobs - delta)).astype(jnp.bfloat16)
    dq = dot(key, dscores, ((0,), (0,))).T * score_scale
    dk = dot(dscores, normed, ((1,), (0,)))
    dv = dot(low, grad, ((1,), (0,)))
    for s, span in enumerate(spans):
        part = slice(s * BLOCK, (s + 1) * BLOCK)
        dk_acc[span, :] += dk[part]
        dv_acc[span, :] += dv[part]
    for h in range(heads):
        part = slice(h * BLOCK, (h + 1) * BLOCK)
        a_ref[:, cut[h]] = out[part].astype(jnp.bfloat16)
        x, s, d = raw[h], scales[h], dq[part]
        gain = gq_ref[h : h + 1, :]
        unit = x * s
        gq_acc[h : h + 1, :] += jnp.sum(d * unit, 0, keepdims=True)
        gd = gain * d
        dq_ref[:, cut[h]] = (s * (gd - unit * jnp.mean(unit * gd, -1, keepdims=True))).astype(jnp.bfloat16)

    @pl.when(n == steps - 1)
    def _():
        chunk = 512

        def finish(i, total):
            span = pl.ds(pl.multiple_of(i * chunk, chunk), chunk)
            d = dk_acc[span, :] * score_scale
            dk_ref[span, :] = d.astype(jnp.bfloat16)
            dv_ref[span, :] = dv_acc[span, :].astype(jnp.bfloat16)
            return total + jnp.sum(d * k_ref[span, :].astype(jnp.float32), 0, keepdims=True)

        total = lax.fori_loop(0, dk_acc.shape[0] // chunk, finish, jnp.zeros((1, head), jnp.float32))
        gp_ref[:heads, :] = gq_acc[...]
        gp_ref[heads:, :] = jnp.broadcast_to(total / kg_ref[pl.ds(c, 1), :], (heads, head))


def attend(cols, lists, q, go, k, v, gq, k_gain):
    group, width = q.shape
    tokens, head = k.shape
    heads = width // head
    steps = group // BLOCK
    slots = lists.shape[1]
    step_spec = pl.BlockSpec((BLOCK, width), lambda n, _: (n, 0))
    low = jnp.bfloat16
    flops = 6 * 2 * group * heads * slots * BLOCK * head
    return pl.pallas_call(
        functools.partial(attend_kernel, cols, steps, slots),
        grid_spec=pltpu.PrefetchScalarGridSpec(
            num_scalar_prefetch=1,
            grid=(steps,),
            in_specs=[step_spec, step_spec] + [VMEM] * 4,
            out_specs=(step_spec, step_spec, VMEM, VMEM, VMEM),
            scratch_shapes=[
                pltpu.VMEM((tokens, head), jnp.float32),
                pltpu.VMEM((tokens, head), jnp.float32),
                pltpu.VMEM((heads, head), jnp.float32),
            ],
        ),
        out_shape=(
            jax.ShapeDtypeStruct((group, width), low),
            jax.ShapeDtypeStruct((group, width), low),
            jax.ShapeDtypeStruct((tokens, head), low),
            jax.ShapeDtypeStruct((tokens, head), low),
            jax.ShapeDtypeStruct((2 * heads, head), jnp.float32),
        ),
        compiler_params=pltpu.CompilerParams(vmem_limit_bytes=LIMIT),
        cost_estimate=pl.CostEstimate(flops=flops, bytes_accessed=16 << 20, transcendentals=0),
    )(lists.reshape(-1), q, go, k, v, gq, k_gain)


def scatter_kernel(
    rows,
    cols,
    depth,
    a_ref,
    dq_ref,
    dk_ref,
    dv_ref,
    gp_ref,
    k_ref,
    kg_ref,
    a_out,
    dq_out,
    dk_out,
    dv_out,
    gq_out,
    gk_out,
    k_sum,
    v_sum,
    k_fin,
    v_fin,
    k_land,
    v_land,
    g1,
    g2,
    g3,
    own_sem,
    wide_send,
    wide_recv,
    k_send,
    k_recv,
    v_send,
    v_recv,
    kv_send,
    kv_recv,
    g1_send,
    g1_recv,
    g2_send,
    g2_recv,
    g3_send,
    g3_recv,
):
    dp, z, c = place(cols)
    tok, head = k_ref.shape[0], k_ref.shape[1] // cols
    width = a_ref.shape[1]

    def at(zz, cc):
        return (dp, lax.rem(zz, rows) * cols + lax.rem(cc, cols))

    across = {d: at(z, c + d) for d in range(1, cols)}
    along = {d: at(z + d, c) for d in range(1, rows)}
    over = {d: (lax.rem(dp + d, depth), z * cols + c) for d in range(1, depth)}
    right, left = along[1], along[rows - 1]
    greet(list(across.values()) + list(along.values()) + list(over.values()))

    sub = k_sum.shape[1] // SUBS
    mine = aligned(c, width)
    large, gains = [], []
    ring = {}

    def ring_step(t):
        k_chunk = lax.rem(z + 2 * rows - 1 - t, rows)
        v_chunk = lax.rem(z + 1 + t, rows)
        for s in range(SUBS):
            part = pl.ds(s * sub, sub)
            for name, chunk, ref, sums, send, recv, to in (
                ("k", k_chunk, dk_ref, k_sum, k_send, k_recv, right),
                ("v", v_chunk, dv_ref, v_sum, v_send, v_recv, left),
            ):
                src = ref.at[chunk, part, :]
                if t:
                    ring[name, t - 1, s].wait_recv()
                    src = sums.at[t - 1, part, :]
                    total = src[...].astype(jnp.float32) + ref[chunk, part, :].astype(jnp.float32)
                    src[...] = total.astype(jnp.bfloat16)
                ring[name, t, s] = push(src, sums.at[t, part, :], send.at[t, s], recv.at[t, s], to)

    ring_step(0)
    for d in range(1, cols):
        part = aligned(lax.rem(c + d, cols), tok)
        for i, (src, dst) in enumerate(((a_ref, a_out), (dq_ref, dq_out))):
            large.append(
                push(src.at[part, :], dst.at[:, mine], wide_send.at[i, d], wide_recv.at[i, d], across[d])
            )
    for i, (src, dst) in enumerate(((a_ref, a_out), (dq_ref, dq_out))):
        large.append(move(src.at[aligned(c, tok), :], dst.at[:, mine], own_sem.at[i]))

    one = [push(gp_ref, g1.at[z], g1_send.at[d], g1_recv.at[d], along[d]) for d in range(1, rows)]
    ring_step(1)
    for copy in one:
        copy.wait()
    g1[z] = gp_ref[...]
    g2[dp] = jnp.sum(g1[...], 0)
    two = [push(g2.at[dp], g2.at[dp], g2_send.at[d], g2_recv.at[d], over[d]) for d in range(1, depth)]
    ring_step(2)
    for copy in two:
        copy.wait()
    g3[c] = jnp.sum(g2[...], 0)
    three = [push(g3.at[c], g3.at[c], g3_send.at[d], g3_recv.at[d], across[d]) for d in range(1, cols)]
    for t in range(3, rows - 1):
        ring_step(t)
    for copy in three:
        copy.wait()
    gq_out[...] = g3[z, pl.ds(c, 1), :]
    gk_out[...] = jnp.concatenate([g3[i, cols : cols + 1, :] for i in range(cols)], axis=0)

    last = rows - 2
    for s in range(SUBS):
        part = pl.ds(s * sub, sub)
        for name, ref, sums, fin in (("k", dk_ref, k_sum, k_fin), ("v", dv_ref, v_sum, v_fin)):
            ring[name, last, s].wait_recv()
            total = sums[last, part, :].astype(jnp.float32) + ref[z, part, :].astype(jnp.float32)
            fin[part, :] = total.astype(jnp.bfloat16)
    back = []
    for d in range(1, cols):
        part = aligned(lax.rem(c + d, cols), tok)
        for i, (fin, land) in enumerate(((k_fin, k_land), (v_fin, v_land))):
            back.append(push(fin.at[part, :], land.at[c], kv_send.at[i, d], kv_recv.at[i, d], across[d]))
    for copy in back:
        copy.wait()
    k_land[c] = k_fin[aligned(c, tok), :]
    v_land[c] = v_fin[aligned(c, tok), :]
    for i in range(cols):
        cut = slice(i * head, (i + 1) * head)
        raw = k_ref[:, cut].astype(jnp.float32)
        scale = lax.rsqrt(jnp.mean(raw * raw, -1, keepdims=True) + EPSILON)
        unit = raw * scale
        gd = kg_ref[i : i + 1, :] * k_land[i].astype(jnp.float32)
        dk_out[:, cut] = (scale * (gd - unit * jnp.mean(unit * gd, -1, keepdims=True))).astype(jnp.bfloat16)
        dv_out[:, cut] = v_land[i]
    for copy in ring.values():
        copy.wait_send()
    for copy in large:
        copy.wait()


def scatter(rows, cols, depth, a, dq, dk, dv, gp, keys, k_gain):
    tok = keys.shape[0]
    head = keys.shape[1] // cols
    group, width = a.shape
    sem = pltpu.SemaphoreType.DMA
    low = jnp.bfloat16
    return pl.pallas_call(
        functools.partial(scatter_kernel, rows, cols, depth),
        out_shape=(
            jax.ShapeDtypeStruct((tok, width * cols), low),
            jax.ShapeDtypeStruct((tok, width * cols), low),
            jax.ShapeDtypeStruct((tok, head * cols), low),
            jax.ShapeDtypeStruct((tok, head * cols), low),
            jax.ShapeDtypeStruct((1, head), jnp.float32),
            jax.ShapeDtypeStruct((cols, head), jnp.float32),
        ),
        in_specs=[ANY] * 2 + [VMEM] * 5,
        out_specs=(ANY, ANY, VMEM, VMEM, VMEM, VMEM),
        scratch_shapes=[
            pltpu.VMEM((rows - 1, group, head), low),
            pltpu.VMEM((rows - 1, group, head), low),
            pltpu.VMEM((group, head), low),
            pltpu.VMEM((group, head), low),
            pltpu.VMEM((cols, tok, head), low),
            pltpu.VMEM((cols, tok, head), low),
            pltpu.VMEM((rows, 2 * cols, head), jnp.float32),
            pltpu.VMEM((depth, 2 * cols, head), jnp.float32),
            pltpu.VMEM((cols, 2 * cols, head), jnp.float32),
            sem((2,)),
            sem((2, cols)),
            sem((2, cols)),
            sem((rows, SUBS)),
            sem((rows, SUBS)),
            sem((rows, SUBS)),
            sem((rows, SUBS)),
            sem((2, cols)),
            sem((2, cols)),
            sem((rows,)),
            sem((rows,)),
            sem((depth,)),
            sem((depth,)),
            sem((cols,)),
            sem((cols,)),
        ],
        compiler_params=pltpu.CompilerParams(
            collective_id=1, has_side_effects=True, vmem_limit_bytes=LIMIT
        ),
        cost_estimate=pl.CostEstimate(flops=0, bytes_accessed=16 << 20, transcendentals=0),
    )(a, dq, dk.reshape(rows, group, head), dv.reshape(rows, group, head), gp, keys, k_gain)


def on_device(depth, queries, keys, values, grad_out, q_gain, k_gain, block_lists):
    cols = k_gain.shape[0]
    rows = lax.axis_size("seq") // cols
    q, go, k, v, gq = gather(rows, cols, queries[0], grad_out[0], keys[0], values[0], q_gain, k_gain)
    head = k.shape[2]
    a, dq, dk, dv, gp = attend(
        cols, block_lists[0], q, go, k.reshape(-1, head), v.reshape(-1, head), gq, k_gain
    )
    a, dq, dk, dv, gain_q, gain_k = scatter(rows, cols, depth, a, dq, dk, dv, gp, keys[0], k_gain)
    return a[None], dq[None], dk[None], dv[None], gain_q, gain_k


def solution(mesh):
    spec = P("dp", "seq", None)
    return jax.shard_map(
        functools.partial(on_device, mesh.shape["dp"]),
        mesh=mesh,
        in_specs=(spec, spec, spec, spec, P("seq", None), P(), P("dp", None, None)),
        out_specs=(spec, spec, spec, spec, P("seq", None), P()),
        check_vma=False,
    )
```

time: 1190 us -> 177 us (0.15); the launches traced: 1170 us -> 176 us
  other arithmetic: 382 us -> 0 us
  waiting for transfers between devices: 276 us -> 0 us
  local copies, waits for them, and re-layouts: 179 us -> 8.56 us
  Pallas kernels: 0 us -> 167 us
  matrix products: 162 us -> 0 us
  blocking collectives: 92.9 us -> 0 us
  starting transfers between devices: 63.8 us -> 0 us
  loops' own time: 12.3 us -> 0 us
    scatter-add x32 -> x0, other arithmetic: 289 us -> none  [the longest x16 145 us: backward_core(): value_total.at[listed].add(value_terms)]
    all_to_all x8 -> x0, waiting for transfers between devices: 276 us -> none  [the longest x1 47.1 us: on_device(): lax.all_to_all(query_send, 'seq', split_axis=1, concat_axis=0, tiled=True)]
    pallas_call x0 -> x3, Pallas kernels: none -> 167 us  [the longest x1 71.6 us: scatter(): pl.pallas_call(functools.partial(scatter_kernel, rows, cols, depth), out_...]
    dot_general x64 -> x0, matrix products: 113 us -> none  [the longest x16 41 us: backward_core(): jnp.einsum('nhikj,nkjhd->nihd', dscores, key_block, preferred_element_typ...]
    psum x2 -> x0, blocking collectives: 92.9 us -> none  [the longest x1 82.6 us: on_device(): gain_k_grad = lax.psum(key_rows, ('dp', 'seq'))]
    unnamed x41 -> x17, local copies, waits for them, and re-layouts: 80.8 us -> 7.88 us
    gather x34 -> x0, local copies, waits for them, and re-layouts: 68.2 us -> none  [the longest x32 64 us: block_inputs(): return (listed, query_block, key_tiles[listed], value_tiles[listed])]
    all_to_all x8 -> x0, starting transfers between devices: 63.8 us -> none  [the longest x1 13 us: on_device(): lax.all_to_all(key_send, 'seq', split_axis=1, concat_axis=0, tiled=True)]
  transfers between devices with their start and end apart: 8 -> 0, of which waited for: 7 -> 0; matrix products, arithmetic and copies ran while one was open for 10% -> 0% of each run, Pallas kernels for 0% -> 0%
where the time goes in v1:
time: 177 us; the launch traced here: 176 us
  Pallas kernels  167 us (94%)
  local copies, waits for them, and re-layouts  8.56 us (5%)
    pallas_call x1, Pallas kernels, scatter(): pl.pallas_call(functools.partial(scatter_kernel, rows, cols, depth), out_...  71.6 us
    pallas_call x1, Pallas kernels, gather(): pl.pallas_call(functools.partial(gather_kernel, rows, cols), out_shape=(j...  64.1 us
    pallas_call x1, Pallas kernels, attend(): pl.pallas_call(functools.partial(attend_kernel, cols, steps, slots), grid...  31.3 us
    unnamed x17, local copies, waits for them, and re-layouts  7.88 us

profile of v1, /device:TPU:1, one launch (start us, length us, event | category | flops | bytes accessed | tf_op | source)
XLA Modules:
  0.0 176.3 jit_solution(18286270410416850653)
XLA Ops:
  0.6 0.8 copy.13
  1.4 0.7 reshape_squeeze.3.lists_ref
  2.1 64.1 %shard_map.118 = (bf16[1024,1024]{1,0:T(8,128)(2,1)}, bf16[1024,1024]{1,0:T(8,128)(2,1)}, bf16[8,1024,128]{2,1,0:T(8,128)(2,1)}, bf16[8,1024,128]{2,1,0:T(8,128)(2,1)}, f32[8,128]{1,0:T(8,128)}) custom-call(bf16[128,8192]{1,0:T(8,128)(2,1)} %bitcast.14, bf16[128,8192]{1,0:T(8,128)(2,1)} %bitcast.15, bf16[128,1024]{1,0:T(8,128)(2,1)} %bitcast.18, ...), custom_call_target="tpu_custom_call" | custom-call | bytes 16777216 | tf_op jit(solution)/shard_map/pallas_call | solution.py:167
  66.2 31.3 %shard_map.119 = (bf16[1024,1024]{1,0:T(8,128)(2,1)}, bf16[1024,1024]{1,0:T(8,128)(2,1)}, bf16[8192,128]{1,0:T(8,128)(2,1)}, bf16[8192,128]{1,0:T(8,128)(2,1)}, f32[16,128]{1,0:T(8,128)}) custom-call(s32[1024]{0:T(1024)} %reshape_squeeze.3.lists_ref, bf16[1024,1024]{1,0:T(8,128)(2,1)} %get-tuple-element.22.q_ref, ...), custom_call_target="tpu_custom_call" | custom-call | flops 6442450944 | bytes 16777216 | tf_op jit(solution)/shard_map/pallas_call | solution.py:305
  97.6 71.6 %shard_map.120 = (bf16[128,8192]{1,0:T(8,128)(2,1)}, bf16[128,8192]{1,0:T(8,128)(2,1)}, bf16[128,1024]{1,0:T(8,128)(2,1)}, bf16[128,1024]{1,0:T(8,128)(2,1)}, f32[1,128]{1,0:T(1,128)}, /*index=5*/f32[8,128]{1,0:T(8,128)}) custom-call(bf16[1024,1024]{1,0:T(8,128)(2,1)} %get-tuple-element.27.a_ref, bf16[1024,1024]{1,0:T(8,128)(2,1)} %get-tuple-element.28.dq_ref, ...), custom_call_target="tpu_custom_call" | custom-call | bytes 16777216 | tf_op jit(solution)/shard_map/pallas_call | solution.py:472
  169.2 0.0 copy-start
  169.2 3.2 %copy.20 = bf16[1,128,8192]{2,1,0:T(8,128)(2,1)} copy(bf16[1,128,8192]{2,1,0:T(8,128)(2,1)} %bitcast.17) | data formatting | bytes 4194304
  172.4 0.0 copy-done
  172.4 0.0 copy-start.2
  172.4 0.0 copy-start.1
  172.4 0.0 copy-start.4
  172.4 0.0 copy-start.3
  172.4 1.3 copy.21
  173.8 0.0 copy-done.2
  173.8 0.7 copy.22
  174.5 0.0 copy-done.1
  174.5 0.7 copy.23
  175.2 0.0 copy-done.4
  175.2 0.5 copy.24
  175.7 0.0 copy-done.3
  175.7 0.6 copy.25
Async XLA Ops:
  169.2 3.3 %copy-start = (bf16[128,8192]{1,0:T(8,128)(2,1)S(1)}, bf16[128,8192]{1,0:T(8,128)(2,1)}, u32[]{:S(2)}) copy-start(bf16[128,8192]{1,0:T(8,128)(2,1)} %get-tuple-element.33) | copy-start | bytes 6291460
  172.4 1.3 copy-start.2
  172.4 2.0 %copy-start.1 = (bf16[128,1024]{1,0:T(8,128)(2,1)S(1)}, bf16[128,1024]{1,0:T(8,128)(2,1)}, u32[]{:S(2)}) copy-start(bf16[128,1024]{1,0:T(8,128)(2,1)} %get-tuple-element.35) | copy-start | bytes 786436
  172.4 2.8 %copy-start.4 = (f32[1,128]{1,0:T(1,128)S(1)}, f32[1,128]{1,0:T(1,128)}, u32[]{:S(2)}) copy-start(f32[1,128]{1,0:T(1,128)} %get-tuple-element.48) | copy-start | bytes 1540
  172.4 3.3 %copy-start.3 = (f32[8,128]{1,0:T(8,128)S(1)}, f32[8,128]{1,0:T(8,128)}, u32[]{:S(2)}) copy-start(f32[8,128]{1,0:T(8,128)} %get-tuple-element.49) | copy-start | bytes 12292

commit v2 on v0

v2 whole, which is shorter than its diff:
```python
import functools
import math

import jax
import jax.numpy as jnp
from jax import lax
from jax.experimental import pallas as pl
from jax.experimental.pallas import tpu as pltpu
from jax.sharding import PartitionSpec as P

EPSILON = 1e-06
BLOCK = 64
SUBS = 2
MESH = pl.DeviceIdType.MESH
ANY = pl.BlockSpec(memory_space=pl.ANY)
VMEM = pl.BlockSpec(memory_space=pltpu.VMEM)
LIMIT = 60 * 1024 * 1024
WINDOW, GLOBALS = 3, 2


def place(cols):
    seq = lax.axis_index("seq")
    return lax.axis_index("dp"), seq // cols, seq % cols


def greet(devices):
    barrier = pltpu.get_barrier_semaphore()
    for device in devices:
        pl.semaphore_signal(barrier, inc=1, device_id=device, device_id_type=MESH)
    pl.semaphore_wait(barrier, len(devices))


def wire(src, dst, send_sem, recv_sem, device):
    return pltpu.make_async_remote_copy(
        src_ref=src,
        dst_ref=dst,
        send_sem=send_sem,
        recv_sem=recv_sem,
        device_id=device,
        device_id_type=MESH,
    )


def push(*args):
    copy = wire(*args)
    copy.start()
    return copy


def move(src, dst, sem):
    copy = pltpu.make_async_copy(src, dst, sem)
    copy.start()
    return copy


def aligned(index, size):
    return pl.ds(pl.multiple_of(index * size, size), size)


def dot(a, b, dims):
    return lax.dot_general(a, b, (dims, ((), ())), preferred_element_type=jnp.float32)


def kernel(
    rows,
    cols,
    depth,
    randoms,
    table,
    q_ref,
    go_ref,
    k_ref,
    v_ref,
    key_ref,
    qg_ref,
    kg_ref,
    a_out,
    dq_out,
    dk_out,
    dv_out,
    gq_out,
    gk_out,
    qx,
    gox,
    kx,
    kall,
    vall,
    gain,
    gx,
    gz,
    qn,
    probs,
    dk_base,
    dv_base,
    dk_rand,
    dv_rand,
    gq_acc,
    gk_acc,
    ax,
    dqx,
    k_sum,
    v_sum,
    k_fin,
    v_fin,
    k_land,
    v_land,
    g1,
    g2,
    g3,
    own_sem,
    in_send,
    in_recv,
    kv_send,
    kv_recv,
    gx_send,
    gx_recv,
    k_send,
    k_recv,
    v_send,
    v_recv,
    gz_send,
    gz_recv,
    out_send,
    out_recv,
    dk_send,
    dk_recv,
    dv_send,
    dv_recv,
    back_send,
    back_recv,
    g1_send,
    g1_recv,
    g2_send,
    g2_recv,
    g3_send,
    g3_recv,
):
    dp, z, c = place(cols)
    tok = q_ref.shape[0]
    width = q_ref.shape[1] // cols
    head = k_ref.shape[1] // cols
    heads = width // head
    group = cols * tok
    per = tok // BLOCK
    steps = group // BLOCK
    blocks = rows * steps
    sub = group // (2 * SUBS)
    score_scale = 1.0 / math.sqrt(head)
    low = jnp.bfloat16
    first_prev, first_last = steps * randoms, 2 * steps * randoms

    def at(zz, cc):
        return (dp, lax.rem(zz, rows) * cols + lax.rem(cc, cols))

    across = {d: at(z, c + d) for d in range(1, cols)}
    along = {d: at(z + d, c) for d in range(1, rows)}
    over = {d: (lax.rem(dp + d, depth), z * cols + c) for d in range(1, depth)}
    right, left = along[1], along[rows - 1]
    mine = aligned(c, tok)
    mine_wide = aligned(c, width)
    parts = [(h, s, h * SUBS + s) for s in range(SUBS) for h in range(2)]

    gain[...] = jnp.broadcast_to(qg_ref[...], gain.shape)
    greet(list(across.values()) + list(along.values()) + list(over.values()))

    small, local = [], []
    for d in range(1, cols):
        part = aligned(lax.rem(c + d, cols), head)
        small.append(push(k_ref.at[:, part], kx.at[mine, :], kv_send.at[0, d], kv_recv.at[0, d], across[d]))
        small.append(push(gain, gx.at[c], gx_send.at[d], gx_recv.at[d], across[d]))
    own_blocks = pl.ds(z * steps + c * per, per)
    late = []
    for d in range(1, cols):
        part = aligned(lax.rem(c + d, cols), head)
        late.append(push(v_ref.at[:, :, part], vall.at[own_blocks], kv_send.at[1, d], kv_recv.at[1, d], across[d]))
    own_k = move(k_ref.at[:, aligned(c, head)], kx.at[mine, :], own_sem.at[0])
    own_v = move(v_ref.at[:, :, aligned(c, head)], vall.at[own_blocks], own_sem.at[1])

    def bring(i, src, dst, d):
        part = aligned(lax.rem(c + d, cols), width)
        return push(src.at[:, part], dst.at[mine, :], in_send.at[i, d], in_recv.at[i, d], across[d])

    q_in = [bring(0, q_ref, qx, d) for d in range(1, cols)]
    own_q = move(q_ref.at[:, mine_wide], qx.at[mine, :], own_sem.at[2])
    own_go = move(go_ref.at[:, mine_wide], gox.at[mine, :], own_sem.at[3])
    for ref in (dk_base, dv_base, gq_acc, gk_acc):
        ref[...] = jnp.zeros_like(ref)
    for ref in (dk_rand, dv_rand, k_sum, v_sum):
        ref[0] = jnp.zeros(ref.shape[1:], ref.dtype)

    own_k.wait()
    for copy in small:
        copy.wait()
    raw_key = kx[...].astype(jnp.float32)
    scale = lax.rsqrt(jnp.mean(raw_key * raw_key, -1, keepdims=True) + EPSILON)
    normed_key = (raw_key * scale * kg_ref[pl.ds(c, 1), :]).astype(low)
    kall[pl.ds(z * steps, steps)] = normed_key.reshape(steps, BLOCK, head)
    gx[c] = gain[...]
    gz[z] = jnp.concatenate([gx[i, :1, :] for i in range(cols)], axis=0)

    def gather(ref, send, recv, t, h, i):
        slot = lax.rem(z + t, rows) if h else lax.rem(z + rows - t, rows)
        part = pl.ds(slot * steps + i * (sub // BLOCK), sub // BLOCK)
        return wire(ref.at[part], ref.at[part], send.at[t, i], recv.at[t, i], left if h else right)

    def gather_step(ref, send, recv, t, waits=True):
        for h, _, i in parts:
            if waits:
                gather(ref, send, recv, t - 1, h, i).wait_recv()
            gather(ref, send, recv, t, h, i).start()

    k_ring, v_ring = (kall, k_send, k_recv), (vall, v_send, v_recv)

    def gain_copy(t):
        slot = lax.rem(z + rows - t, rows)
        return wire(gz.at[slot], gz.at[slot], gz_send.at[t], gz_recv.at[t], right)

    lag = rows // 2
    go_in = []
    for t in range(rows - 1):
        gather_step(*k_ring, t, t > 0)
        if t:
            gain_copy(t - 1).wait_recv()
        gain_copy(t).start()
        if t == 1:
            own_v.wait()
            for copy in late:
                copy.wait()
        if t >= lag:
            gather_step(*v_ring, t - lag, t > lag)
            more = -(-(cols - 1) // (rows - 1 - lag))
            for d in range(cols - 1, 0, -1)[(t - lag) * more : (t - lag + 1) * more]:
                go_in.append(bring(1, go_ref, gox, d))
    for h, _, i in parts:
        gather(*k_ring, rows - 2, h, i).wait_recv()
    gain_copy(rows - 2).wait_recv()
    own_q.wait()
    for copy in q_in:
        copy.wait()

    cut = [slice(h * head, (h + 1) * head) for h in range(heads)]
    gains = [gz[c, h : h + 1, :] for h in range(heads)]

    def block_of(i):
        return lax.rem(per * (c + 1) + i, steps)

    def fixed(n):
        return [lax.rem(z * steps + n + s + blocks - WINDOW // 2, blocks) for s in range(WINDOW)] + list(range(GLOBALS))

    def listed(ref, i, n):
        ids = fixed(n) + [table[i * randoms + s] for s in range(randoms)]
        return jnp.concatenate([ref[b] for b in ids], axis=0)

    def unit_queries(n):
        raw = [qx[aligned(n, BLOCK), s].astype(jnp.float32) for s in cut]
        scales = [lax.rsqrt(jnp.mean(x * x, -1, keepdims=True) + EPSILON) for x in raw]
        return [x * s for x, s in zip(raw, scales)], scales

    def cotangents(n):
        return jnp.concatenate([gox[aligned(n, BLOCK), s] for s in cut], axis=0)

    def spread(base, rand, i, n, terms):
        for s, b in enumerate(fixed(n)):
            base[aligned(b, BLOCK), :] += terms[s * BLOCK : (s + 1) * BLOCK]
        for s in range(randoms):
            m = i * randoms + s
            first = (WINDOW + GLOBALS + s) * BLOCK
            rand[m + 1] = rand[table[first_prev + m]] + terms[first : first + BLOCK]

    def make_probs(i):
        n = block_of(i)
        units, _ = unit_queries(n)
        normed = jnp.concatenate([(u * g).astype(low) for u, g in zip(units, gains)], axis=0)
        qn[n] = normed
        scores = dot(normed, listed(kall, i, n), ((1,), (1,)))
        expo = jnp.exp2(scores * (score_scale * math.log2(math.e)))
        probs[n] = (expo * (1.0 / jnp.sum(expo, axis=1, keepdims=True))).astype(low)

    def make_dv(i):
        n = block_of(i)
        spread(dv_base, dv_rand, i, n, dot(probs[n], cotangents(n), ((0,), (0,))))

    def make_rest(i):
        n = block_of(i)
        key, value, grad, prob = listed(kall, i, n), listed(vall, i, n), cotangents(n), probs[n]
        out = dot(prob, value, ((1,), (0,)))
        dprobs = dot(grad, value, ((1,), (1,)))
        delta = jnp.sum(out * grad.astype(jnp.float32), axis=1, keepdims=True)
        dscores = (prob.astype(jnp.float32) * (dprobs - delta)).astype(low)
        dq = dot(dscores, key, ((1,), (0,))) * score_scale
        dk = dot(dscores, qn[n], ((0,), (0,))) * score_scale
        spread(dk_base, dk_rand, i, n, dk)
        gk_acc[...] += jnp.sum(dk * key.astype(jnp.float32), axis=0, keepdims=True)
        units, scales = unit_queries(n)
        for h in range(heads):
            part = slice(h * BLOCK, (h + 1) * BLOCK)
            ax[aligned(n, BLOCK), cut[h]] = out[part].astype(low)
            d, unit = dq[part], units[h]
            gq_acc[h : h + 1, :] += jnp.sum(d * unit, 0, keepdims=True)
            gd = gains[h] * d
            dqx[aligned(n, BLOCK), cut[h]] = (
                scales[h] * (gd - unit * jnp.mean(unit * gd, -1, keepdims=True))
            ).astype(low)

    def pair(work, j):
        for p in range(per):
            work(j * per + p)

    early = rows - 1 - lag
    share = cols // (rows - 1 - early)

    def probs_step(u, _):
        gather_step(*v_ring, u + early)
        for w in range(share):
            pair(make_probs, u * share + w)
        return 0

    lax.fori_loop(0, rows - 1 - early, probs_step, 0)

    own_go.wait()
    for copy in go_in:
        copy.wait()

    def dv_step(j, _):
        pair(make_dv, j)
        return 0

    lax.fori_loop(0, cols, dv_step, 0)
    for h, _, i in parts:
        gather(*v_ring, rows - 2, h, i).wait_recv()

    def reduce(sums, send, recv, t, h, i):
        part = pl.ds(i * sub, sub)
        return wire(sums.at[t, part, :], sums.at[t + 1, part, :], send.at[t, i], recv.at[t, i], left if h else right)

    def own_part(base, rand, chunk, i):
        start = chunk * group + i * sub
        return jnp.concatenate(
            [
                base[pl.ds(pl.multiple_of(start + b * BLOCK, BLOCK), BLOCK), :]
                + rand[table[first_last + chunk * steps + i * (sub // BLOCK) + b]]
                for b in range(sub // BLOCK)
            ],
            axis=0,
        )

    def reduce_step(base, rand, sums, send, recv, t, waits):
        for h, _, i in parts:
            chunk = lax.rem(z + 1 + t, rows) if h else lax.rem(z + 2 * rows - 1 - t, rows)
            own = own_part(base, rand, chunk, i)
            if waits is True:
                reduce(sums, send, recv, t - 1, h, i).wait_recv()
            elif waits is not False:

                @pl.when(waits)
                def _():
                    reduce(sums, send, recv, t - 1, h, i).wait_recv()

            part = pl.ds(i * sub, sub)
            sums[t, part, :] = (sums[t, part, :].astype(jnp.float32) + own).astype(low)
            reduce(sums, send, recv, t, h, i).start()

    def finish(base, rand, sums, send, recv, fin, land, w):
        copies = []
        for h, _, i in parts:
            own = own_part(base, rand, z, i)
            reduce(sums, send, recv, rows - 2, h, i).wait_recv()
            part = pl.ds(i * sub, sub)
            fin[part, :] = (sums[rows - 1, part, :].astype(jnp.float32) + own).astype(low)
        for d in range(1, cols):
            part = aligned(lax.rem(c + d, cols), tok)
            copies.append(push(fin.at[part, :], land.at[c], back_send.at[w, d], back_recv.at[w, d], across[d]))
        return copies

    dk_ring = (dk_base, dk_rand, k_sum, dk_send, dk_recv)
    dv_ring = (dv_base, dv_rand, v_sum, dv_send, dv_recv)

    def give(i, src, dst, j):
        part = aligned(lax.rem(c + 1 + j, cols), tok)
        to = at(z, c + 1 + j)
        return wire(src.at[part, :], dst.at[:, mine_wide], out_send.at[i, j], out_recv.at[i, j], to)

    outs = ((0, ax, a_out), (1, dqx, dq_out))

    def rest_step(u, _):
        reduce_step(*dv_ring, u, u > 0)
        for w in range(share):
            j = u * share + w
            pair(make_rest, j)

            @pl.when(j < cols - 1)
            def _():
                for out in outs:
                    give(*out, j).start()

        return 0

    lax.fori_loop(0, rows - 1 - early, rest_step, 0)
    for i, src, dst in outs:
        local.append(move(src.at[mine, :], dst.at[:, mine_wide], own_sem.at[4 + i]))
    gp = g1.at[z]
    gp[:heads, :] = gq_acc[...]
    gp[heads:, :] = jnp.broadcast_to(gk_acc[...] / kg_ref[pl.ds(c, 1), :], (heads, head))

    reduce_step(*dk_ring, 0, False)
    one = [push(gp, gp, g1_send.at[d], g1_recv.at[d], along[d]) for d in range(1, rows)]
    reduce_step(*dv_ring, rows - 1 - early, True)

    def both_step(u, _):
        reduce_step(*dk_ring, u, True)
        reduce_step(*dv_ring, u + rows - 1 - early, True)
        return 0

    lax.fori_loop(1, early, both_step, 0)
    for copy in one:
        copy.wait()
    g2[dp] = jnp.sum(g1[...], 0)
    two = [push(g2.at[dp], g2.at[dp], g2_send.at[d], g2_recv.at[d], over[d]) for d in range(1, depth)]
    back = finish(*dv_ring, v_fin, v_land, 1)

    def dk_step(u, _):
        reduce_step(*dk_ring, u, True)
        return 0

    lax.fori_loop(early, rows - 2, dk_step, 0)
    for copy in two:
        copy.wait()
    g3[c] = jnp.sum(g2[...], 0)
    three = [push(g3.at[c], g3.at[c], g3_send.at[d], g3_recv.at[d], across[d]) for d in range(1, cols)]
    reduce_step(*dk_ring, rows - 2, True)
    for copy in back:
        copy.wait()
    v_land[c] = v_fin[mine, :]
    for i in range(cols):
        dv_out[:, cut[i]] = v_land[i]
    back = finish(*dk_ring, k_fin, k_land, 0)

    for copy in three:
        copy.wait()
    gq_out[...] = g3[z, pl.ds(c, 1), :]
    gk_out[...] = jnp.concatenate([g3[i, cols : cols + 1, :] for i in range(cols)], axis=0)
    k_land[c] = k_fin[mine, :]
    for copy in back:
        copy.wait()
    for i in range(cols):
        raw = key_ref[:, cut[i]].astype(jnp.float32)
        scale = lax.rsqrt(jnp.mean(raw * raw, -1, keepdims=True) + EPSILON)
        unit = raw * scale
        gd = kg_ref[i : i + 1, :] * k_land[i].astype(jnp.float32)
        dk_out[:, cut[i]] = (scale * (gd - unit * jnp.mean(unit * gd, -1, keepdims=True))).astype(low)

    for t in range(rows - 1):
        gain_copy(t).wait_send()
        for h, _, i in parts:
            gather(*k_ring, t, h, i).wait_send()
            gather(*v_ring, t, h, i).wait_send()
            reduce(*dk_ring[2:], t, h, i).wait_send()
            reduce(*dv_ring[2:], t, h, i).wait_send()
    for j in range(cols - 1):
        for out in outs:
            give(*out, j).wait()
    for copy in local:
        copy.wait()


def make_table(rows, cols, per, lists):
    _, z, c = place(cols)
    steps = cols * per
    here = lax.dynamic_slice_in_dim(lists, z * steps, steps, 0)[:, WINDOW + GLOBALS :]
    turned = lax.dynamic_slice_in_dim(jnp.concatenate([here, here]), per * (c + 1) % steps, steps, 0).reshape(-1)
    order = jnp.arange(turned.shape[0], dtype=jnp.int32)
    same = (turned[:, None] == turned[None, :]) & (order[None, :] < order[:, None])
    prev = jnp.max(jnp.where(same, order[None, :] + 1, 0), axis=1)
    ids = jnp.arange(lists.shape[0], dtype=jnp.int32)
    last = jnp.max(jnp.where(ids[:, None] == turned[None, :], order[None, :] + 1, 0), axis=1)
    return jnp.concatenate([turned, prev, last]).astype(jnp.int32)


def on_device(depth, queries, keys, values, grad_out, q_gain, k_gain, block_lists):
    cols = k_gain.shape[0]
    rows = lax.axis_size("seq") // cols
    _, tok, wide = queries.shape
    head = q_gain.shape[1]
    width = wide // cols
    heads = width // head
    group = cols * tok
    steps = group // BLOCK
    lists = block_lists[0]
    randoms = lists.shape[1] - WINDOW - GLOBALS
    table = make_table(rows, cols, tok // BLOCK, lists)
    low, full = jnp.bfloat16, jnp.float32
    sem = pltpu.SemaphoreType.DMA
    ring = (rows, 2 * SUBS)
    tile = 2 * heads
    flops = 6 * 2 * group * heads * lists.shape[1] * BLOCK * head
    a, dq, dk, dv, gain_q, gain_k = pl.pallas_call(
        functools.partial(kernel, rows, cols, depth, randoms),
        out_shape=(
            jax.ShapeDtypeStruct((tok, wide), low),
            jax.ShapeDtypeStruct((tok, wide), low),
            jax.ShapeDtypeStruct((tok, head * cols), low),
            jax.ShapeDtypeStruct((tok, head * cols), low),
            jax.ShapeDtypeStruct((1, head), full),
            jax.ShapeDtypeStruct((cols, head), full),
        ),
        in_specs=[pl.BlockSpec(memory_space=pltpu.SMEM)] + [ANY] * 4 + [VMEM] * 3,
        out_specs=(ANY, ANY, VMEM, VMEM, VMEM, VMEM),
        scratch_shapes=[
            pltpu.VMEM((group, width), low),
            pltpu.VMEM((group, width), low),
            pltpu.VMEM((group, head), low),
            pltpu.VMEM((rows * steps, BLOCK, head), low),
            pltpu.VMEM((rows * steps, BLOCK, head), low),
            pltpu.VMEM((8, head), full),
            pltpu.VMEM((cols, 8, head), full),
            pltpu.VMEM((rows, cols, head), full),
            pltpu.VMEM((steps, heads * BLOCK, head), low),
            pltpu.VMEM((steps, heads * BLOCK, lists.shape[1] * BLOCK), low),
            pltpu.VMEM((rows * group, head), full),
            pltpu.VMEM((rows * group, head), full),
            pltpu.VMEM((steps * randoms + 1, BLOCK, head), full),
            pltpu.VMEM((steps * randoms + 1, BLOCK, head), full),
            pltpu.VMEM((heads, head), full),
            pltpu.VMEM((1, head), full),
            pltpu.VMEM((group, width), low),
            pltpu.VMEM((group, width), low),
            pltpu.VMEM((rows, group, head), low),
            pltpu.VMEM((rows, group, head), low),
            pltpu.VMEM((group, head), low),
            pltpu.VMEM((group, head), low),
            pltpu.VMEM((cols, tok, head), low),
            pltpu.VMEM((cols, tok, head), low),
            pltpu.VMEM((rows, tile, head), full),
            pltpu.VMEM((depth, tile, head), full),
            pltpu.VMEM((cols, tile, head), full),
            sem((6,)),
            sem((2, cols)),
            sem((2, cols)),
            sem((2, cols)),
            sem((2, cols)),
            sem((cols,)),
            sem((cols,)),
            sem(ring),
            sem(ring),
            sem(ring),
            sem(ring),
            sem((rows,)),
            sem((rows,)),
            sem((2, cols)),
            sem((2, cols)),
            sem(ring),
            sem(ring),
            sem(ring),
            sem(ring),
            sem((2, cols)),
            sem((2, cols)),
            sem((rows,)),
            sem((rows,)),
            sem((depth,)),
            sem((depth,)),
            sem((cols,)),
            sem((cols,)),
        ],
        compiler_params=pltpu.CompilerParams(
            collective_id=0, has_side_effects=True, vmem_limit_bytes=LIMIT
        ),
        cost_estimate=pl.CostEstimate(flops=flops, bytes_accessed=16 << 20, transcendentals=0),
    )(
        table,
        queries[0],
        grad_out[0],
        keys[0],
        values.reshape(tok // BLOCK, BLOCK, head * cols),
        keys[0],
        q_gain,
        k_gain,
    )
    return a[None], dq[None], dk[None], dv[None], gain_q, gain_k


def solution(mesh):
    spec = P("dp", "seq", None)
    return jax.shard_map(
        functools.partial(on_device, mesh.shape["dp"]),
        mesh=mesh,
        in_specs=(spec, spec, spec, spec, P("seq", None), P(), P("dp", None, None)),
        out_specs=(spec, spec, spec, spec, P("seq", None), P()),
        check_vma=False,
    )
```

time: 1190 us -> 147 us (0.12); the launches traced: 1170 us -> 147 us
  other arithmetic: 382 us -> 1.01 us
  waiting for transfers between devices: 276 us -> 0 us
  local copies, waits for them, and re-layouts: 179 us -> 8.05 us
  matrix products: 162 us -> 0 us
  Pallas kernels: 0 us -> 137 us
  blocking collectives: 92.9 us -> 0 us
  starting transfers between devices: 63.8 us -> 0 us
  loops' own time: 12.3 us -> 0 us
    scatter-add x32 -> x0, other arithmetic: 289 us -> none  [the longest x16 145 us: backward_core(): value_total.at[listed].add(value_terms)]
    all_to_all x8 -> x0, waiting for transfers between devices: 276 us -> none  [the longest x1 47.1 us: on_device(): lax.all_to_all(query_send, 'seq', split_axis=1, concat_axis=0, tiled=True)]
    pallas_call x0 -> x1, Pallas kernels: none -> 137 us  [on_device(): pl.pallas_call(functools.partial(kernel, rows, cols, depth, randoms), out...]
    dot_general x64 -> x0, matrix products: 113 us -> none  [the longest x16 41 us: backward_core(): jnp.einsum('nhikj,nkjhd->nihd', dscores, key_block, preferred_element_typ...]
    psum x2 -> x0, blocking collectives: 92.9 us -> none  [the longest x1 82.6 us: on_device(): gain_k_grad = lax.psum(key_rows, ('dp', 'seq'))]
    unnamed x41 -> x18, local copies, waits for them, and re-layouts: 80.8 us -> 7.72 us
    gather x34 -> x0, local copies, waits for them, and re-layouts: 68.2 us -> none  [the longest x32 64 us: block_inputs(): return (listed, query_block, key_tiles[listed], value_tiles[listed])]
    all_to_all x8 -> x0, starting transfers between devices: 63.8 us -> none  [the longest x1 13 us: on_device(): lax.all_to_all(key_send, 'seq', split_axis=1, concat_axis=0, tiled=True)]
  transfers between devices with their start and end apart: 8 -> 0, of which waited for: 7 -> 0; matrix products, arithmetic and copies ran while one was open for 10% -> 0% of each run, Pallas kernels for 0% -> 0%
where the time goes in v2:
time: 147 us
  Pallas kernels  137 us (93%)
  local copies, waits for them, and re-layouts  8.05 us (5%)
    pallas_call x1, Pallas kernels, on_device(): pl.pallas_call(functools.partial(kernel, rows, cols, depth, randoms), out...  137 us
    unnamed x18, local copies, waits for them, and re-layouts  7.72 us

profile of v2, /device:TPU:1, one launch (start us, length us, event | category | flops | bytes accessed | tf_op | source)
XLA Modules:
  0.0 147.1 jit_solution(7733104404871500624)
XLA Ops:
  0.6 0.0 copy-start
  0.7 0.6 copy-done
  1.3 0.1 dynamic-slice_bitcast_fusion
  1.4 0.1 pad_add_fusion
  1.5 0.1 constant_dynamic-slice_fusion
  1.6 0.1 copy.15
  1.6 0.1 reshape.26
  1.7 0.1 select_reduce_fusion
  1.8 0.2 select_reduce_fusion.1
  2.0 0.6 pad_add_fusion.1.table
  2.7 137.3 %shard_map.118 = (bf16[128,8192]{1,0:T(8,128)(2,1)}, bf16[128,8192]{1,0:T(8,128)(2,1)}, bf16[128,1024]{1,0:T(8,128)(2,1)}, bf16[128,1024]{1,0:T(8,128)(2,1)}, f32[1,128]{1,0:T(1,128)}, /*index=5*/f32[8,128]{1,0:T(8,128)}) custom-call(s32[224]{0:T(256)} %pad_add_fusion.1.table, bf16[128,8192]{1,0:T(8,128)(2,1)} %bitcast.14, bf16[128,8192]{1,0:T(8,128)(2,1)} %bitcast.15, ...), custom_call_target="tpu_custom_call" | custom-call | flops 6442450944 | bytes 16777216 | tf_op jit(solution)/shard_map/pallas_call | solution.py:496
  140.0 0.0 copy-start.1
  140.0 3.2 %copy.22 = bf16[1,128,8192]{2,1,0:T(8,128)(2,1)} copy(bf16[1,128,8192]{2,1,0:T(8,128)(2,1)} %bitcast.11) | data formatting | bytes 4194304
  143.2 0.0 copy-done.1
  143.3 0.0 copy-start.3
  143.3 0.0 copy-start.2
  143.3 0.0 copy-start.5
  143.3 0.0 copy-start.4
  143.3 1.3 copy.23
  144.6 0.0 copy-done.3
  144.6 0.7 copy.24
  145.3 0.0 copy-done.2
  145.3 0.7 copy.25
  146.0 0.0 copy-done.5
  146.0 0.5 copy.26
  146.5 0.0 copy-done.4
  146.5 0.6 copy.27
  (2 shorter events, 0.0 us)
Async XLA Ops:
  0.6 0.7 copy-start
  140.0 3.3 %copy-start.1 = (bf16[128,8192]{1,0:T(8,128)(2,1)S(1)}, bf16[128,8192]{1,0:T(8,128)(2,1)}, u32[]{:S(2)}) copy-start(bf16[128,8192]{1,0:T(8,128)(2,1)} %get-tuple-element.13) | copy-start | bytes 6291460
  143.3 1.3 copy-start.3
  143.3 2.0 %copy-start.2 = (bf16[128,1024]{1,0:T(8,128)(2,1)S(1)}, bf16[128,1024]{1,0:T(8,128)(2,1)}, u32[]{:S(2)}) copy-start(bf16[128,1024]{1,0:T(8,128)(2,1)} %get-tuple-element.15) | copy-start | bytes 786436
  143.3 2.8 %copy-start.5 = (f32[1,128]{1,0:T(1,128)S(1)}, f32[1,128]{1,0:T(1,128)}, u32[]{:S(2)}) copy-start(f32[1,128]{1,0:T(1,128)} %get-tuple-element.28) | copy-start | bytes 1540
  143.3 3.3 %copy-start.4 = (f32[8,128]{1,0:T(8,128)S(1)}, f32[8,128]{1,0:T(8,128)}, u32[]{:S(2)}) copy-start(f32[8,128]{1,0:T(8,128)} %get-tuple-element.29) | copy-start | bytes 12292

commit v3 on v2

--- a/solution.py
+++ b/solution.py
@@ -16,6 +16,8 @@
 VMEM = pl.BlockSpec(memory_space=pltpu.VMEM)
 LIMIT = 60 * 1024 * 1024
 WINDOW, GLOBALS = 3, 2
+LAG, GO_FROM, STRIDE = 2, 3, 3
+PIECES = 2
 
 
 def place(cols):
@@ -71,15 +73,13 @@
     go_ref,
     k_ref,
     v_ref,
-    key_ref,
     qg_ref,
     kg_ref,
     a_out,
     dq_out,
-    dk_out,
-    dv_out,
-    gq_out,
-    gk_out,
+    k_land,
+    v_land,
+    g3,
     qx,
     gox,
     kx,
@@ -88,6 +88,7 @@
     gain,
     gx,
     gz,
+    gq_own,
     qn,
     probs,
     dk_base,
@@ -102,11 +103,9 @@
     v_sum,
     k_fin,
     v_fin,
-    k_land,
-    v_land,
     g1,
     g2,
-    g3,
+    g2_sum,
     own_sem,
     in_send,
     in_recv,
@@ -196,7 +195,15 @@
     normed_key = (raw_key * scale * kg_ref[pl.ds(c, 1), :]).astype(low)
     kall[pl.ds(z * steps, steps)] = normed_key.reshape(steps, BLOCK, head)
     gx[c] = gain[...]
-    gz[z] = jnp.concatenate([gx[i, :1, :] for i in range(cols)], axis=0)
+    gz[...] = jnp.concatenate([gx[i, :1, :] for i in range(cols)], axis=0)
+    served = [wire(gz, gq_own, gz_send.at[d], gz_recv.at[0], along[d]) for d in range(1, rows)]
+
+    @pl.when(z == c)
+    def _():
+        for copy in served:
+            copy.start()
+        gq_own[...] = gz[...]
+
 
     def gather(ref, send, recv, t, h, i):
         slot = lax.rem(z + t, rows) if h else lax.rem(z + rows - t, rows)
@@ -211,44 +218,45 @@
 
     k_ring, v_ring = (kall, k_send, k_recv), (vall, v_send, v_recv)
 
-    def gain_copy(t):
-        slot = lax.rem(z + rows - t, rows)
-        return wire(gz.at[slot], gz.at[slot], gz_send.at[t], gz_recv.at[t], right)
-
-    lag = rows // 2
+    lag, lag_out, go_from = LAG, rows // 2, GO_FROM
     go_in = []
     for t in range(rows - 1):
         gather_step(*k_ring, t, t > 0)
-        if t:
-            gain_copy(t - 1).wait_recv()
-        gain_copy(t).start()
-        if t == 1:
-            own_v.wait()
-            for copy in late:
-                copy.wait()
         if t >= lag:
+            if t == lag:
+                own_v.wait()
+                for copy in late:
+                    copy.wait()
             gather_step(*v_ring, t - lag, t > lag)
-            more = -(-(cols - 1) // (rows - 1 - lag))
-            for d in range(cols - 1, 0, -1)[(t - lag) * more : (t - lag + 1) * more]:
+        if t >= go_from:
+            more = -(-(cols - 1) // (rows - 1 - go_from))
+            for d in [-STRIDE * (j + 1) % cols for j in range(cols - 1)][(t - go_from) * more : (t - go_from + 1) * more]:
                 go_in.append(bring(1, go_ref, gox, d))
     for h, _, i in parts:
         gather(*k_ring, rows - 2, h, i).wait_recv()
-    gain_copy(rows - 2).wait_recv()
+
+    @pl.when(z != c)
+    def _():
+        served[0].wait_recv()
+
     own_q.wait()
     for copy in q_in:
         copy.wait()
 
     cut = [slice(h * head, (h + 1) * head) for h in range(heads)]
-    gains = [gz[c, h : h + 1, :] for h in range(heads)]
+    gains = [gq_own[h : h + 1, :] for h in range(heads)]
+
+    def owner(j):
+        return lax.rem(c + STRIDE * (j + 1), cols)
 
     def block_of(i):
-        return lax.rem(per * (c + 1) + i, steps)
+        return per * owner(i // per) + i % per
 
     def fixed(n):
         return [lax.rem(z * steps + n + s + blocks - WINDOW // 2, blocks) for s in range(WINDOW)] + list(range(GLOBALS))
 
-    def listed(ref, i, n):
-        ids = fixed(n) + [table[i * randoms + s] for s in range(randoms)]
+    def listed(ref, n):
+        ids = fixed(n) + [table[n * randoms + s] for s in range(randoms)]
         return jnp.concatenate([ref[b] for b in ids], axis=0)
 
     def unit_queries(n):
@@ -263,16 +271,15 @@
         for s, b in enumerate(fixed(n)):
             base[aligned(b, BLOCK), :] += terms[s * BLOCK : (s + 1) * BLOCK]
         for s in range(randoms):
-            m = i * randoms + s
             first = (WINDOW + GLOBALS + s) * BLOCK
-            rand[m + 1] = rand[table[first_prev + m]] + terms[first : first + BLOCK]
+            rand[i * randoms + s + 1] = rand[table[first_prev + n * randoms + s]] + terms[first : first + BLOCK]
 
     def make_probs(i):
         n = block_of(i)
         units, _ = unit_queries(n)
         normed = jnp.concatenate([(u * g).astype(low) for u, g in zip(units, gains)], axis=0)
         qn[n] = normed
-        scores = dot(normed, listed(kall, i, n), ((1,), (1,)))
+        scores = dot(normed, listed(kall, n), ((1,), (1,)))
         expo = jnp.exp2(scores * (score_scale * math.log2(math.e)))
         probs[n] = (expo * (1.0 / jnp.sum(expo, axis=1, keepdims=True))).astype(low)
 
@@ -282,7 +289,7 @@
 
     def make_rest(i):
         n = block_of(i)
-        key, value, grad, prob = listed(kall, i, n), listed(vall, i, n), cotangents(n), probs[n]
+        key, value, grad, prob = listed(kall, n), listed(vall, n), cotangents(n), probs[n]
         out = dot(prob, value, ((1,), (0,)))
         dprobs = dot(grad, value, ((1,), (1,)))
         delta = jnp.sum(out * grad.astype(jnp.float32), axis=1, keepdims=True)
@@ -307,16 +314,33 @@
             work(j * per + p)
 
     early = rows - 1 - lag
-    share = cols // (rows - 1 - early)
+    share = cols // lag if lag else cols
+
+    def probs_pair(j):
+        pair(make_probs, j)
+        return 0
 
     def probs_step(u, _):
         gather_step(*v_ring, u + early)
-        for w in range(share):
-            pair(make_probs, u * share + w)
+        lax.fori_loop(0, share, lambda w, _: probs_pair(u * share + w), 0)
         return 0
 
-    lax.fori_loop(0, rows - 1 - early, probs_step, 0)
-
+    if lag:
+        lax.fori_loop(0, lag, probs_step, 0)
+    else:
+        for w in range(cols):
+            pair(make_probs, w)
+
+
+    @pl.when(z == c)
+    def _():
+        for copy in served:
+            copy.wait_send()
+
+    for t in range(rows - 2):
+        for h, _, i in parts:
+            gather(*k_ring, t, h, i).wait_send()
+            gather(*v_ring, t, h, i).wait_send()
     own_go.wait()
     for copy in go_in:
         copy.wait()
@@ -328,6 +352,8 @@
     lax.fori_loop(0, cols, dv_step, 0)
     for h, _, i in parts:
         gather(*v_ring, rows - 2, h, i).wait_recv()
+        gather(*k_ring, rows - 2, h, i).wait_send()
+        gather(*v_ring, rows - 2, h, i).wait_send()
 
     def reduce(sums, send, recv, t, h, i):
         part = pl.ds(i * sub, sub)
@@ -361,26 +387,39 @@
             reduce(sums, send, recv, t, h, i).start()
 
     def finish(base, rand, sums, send, recv, fin, land, w):
-        copies = []
         for h, _, i in parts:
             own = own_part(base, rand, z, i)
             reduce(sums, send, recv, rows - 2, h, i).wait_recv()
             part = pl.ds(i * sub, sub)
             fin[part, :] = (sums[rows - 1, part, :].astype(jnp.float32) + own).astype(low)
+            for cc in range(i * sub // tok, (i + 1) * sub // tok):
+                d = lax.rem(cc - c + cols, cols)
+
+                @pl.when(d > 0)
+                def _():
+                    back(fin, land, w, cc, d).start()
+
+        local.append(move(fin.at[mine, :], land.at[c], own_sem.at[6 + w]))
+
+    def back(fin, land, w, cc, d):
+        return wire(fin.at[pl.ds(cc * tok, tok), :], land.at[c], back_send.at[w, d], back_recv.at[w, d], at(z, cc))
+
+    def finish_wait(fin, land, w):
         for d in range(1, cols):
-            part = aligned(lax.rem(c + d, cols), tok)
-            copies.append(push(fin.at[part, :], land.at[c], back_send.at[w, d], back_recv.at[w, d], across[d]))
-        return copies
+            back(fin, land, w, 0, d).wait()
 
     dk_ring = (dk_base, dk_rand, k_sum, dk_send, dk_recv)
     dv_ring = (dv_base, dv_rand, v_sum, dv_send, dv_recv)
 
     def give(i, src, dst, j):
-        part = aligned(lax.rem(c + 1 + j, cols), tok)
-        to = at(z, c + 1 + j)
+        part = aligned(owner(j), tok)
+        to = at(z, owner(j))
         return wire(src.at[part, :], dst.at[:, mine_wide], out_send.at[i, j], out_recv.at[i, j], to)
 
     outs = ((0, ax, a_out), (1, dqx, dq_out))
+
+    early = rows - 1 - lag_out
+    share = cols // lag_out
 
     def rest_step(u, _):
         reduce_step(*dv_ring, u, u > 0)
@@ -395,7 +434,7 @@
 
         return 0
 
-    lax.fori_loop(0, rows - 1 - early, rest_step, 0)
+    lax.fori_loop(0, lag_out, rest_step, 0)
     for i, src, dst in outs:
         local.append(move(src.at[mine, :], dst.at[:, mine_wide], own_sem.at[4 + i]))
     gp = g1.at[z]
@@ -404,11 +443,11 @@
 
     reduce_step(*dk_ring, 0, False)
     one = [push(gp, gp, g1_send.at[d], g1_recv.at[d], along[d]) for d in range(1, rows)]
-    reduce_step(*dv_ring, rows - 1 - early, True)
+    reduce_step(*dv_ring, lag_out, True)
 
     def both_step(u, _):
         reduce_step(*dk_ring, u, True)
-        reduce_step(*dv_ring, u + rows - 1 - early, True)
+        reduce_step(*dv_ring, u + lag_out, True)
         return 0
 
     lax.fori_loop(1, early, both_step, 0)
@@ -416,7 +455,7 @@
         copy.wait()
     g2[dp] = jnp.sum(g1[...], 0)
     two = [push(g2.at[dp], g2.at[dp], g2_send.at[d], g2_recv.at[d], over[d]) for d in range(1, depth)]
-    back = finish(*dv_ring, v_fin, v_land, 1)
+    finish(*dv_ring, v_fin, v_land, 1)
 
     def dk_step(u, _):
         reduce_step(*dk_ring, u, True)
@@ -425,55 +464,103 @@
     lax.fori_loop(early, rows - 2, dk_step, 0)
     for copy in two:
         copy.wait()
-    g3[c] = jnp.sum(g2[...], 0)
-    three = [push(g3.at[c], g3.at[c], g3_send.at[d], g3_recv.at[d], across[d]) for d in range(1, cols)]
+    g2_sum[...] = jnp.sum(g2[...], 0)
+    three = [push(g2_sum, g3.at[c], g3_send.at[d], g3_recv.at[d], across[d]) for d in range(1, cols)]
+    local.append(move(g2_sum, g3.at[c], own_sem.at[8]))
     reduce_step(*dk_ring, rows - 2, True)
-    for copy in back:
-        copy.wait()
-    v_land[c] = v_fin[mine, :]
-    for i in range(cols):
-        dv_out[:, cut[i]] = v_land[i]
-    back = finish(*dk_ring, k_fin, k_land, 0)
-
-    for copy in three:
-        copy.wait()
-    gq_out[...] = g3[z, pl.ds(c, 1), :]
-    gk_out[...] = jnp.concatenate([g3[i, cols : cols + 1, :] for i in range(cols)], axis=0)
-    k_land[c] = k_fin[mine, :]
-    for copy in back:
-        copy.wait()
-    for i in range(cols):
-        raw = key_ref[:, cut[i]].astype(jnp.float32)
-        scale = lax.rsqrt(jnp.mean(raw * raw, -1, keepdims=True) + EPSILON)
-        unit = raw * scale
-        gd = kg_ref[i : i + 1, :] * k_land[i].astype(jnp.float32)
-        dk_out[:, cut[i]] = (scale * (gd - unit * jnp.mean(unit * gd, -1, keepdims=True))).astype(low)
-
-    for t in range(rows - 1):
-        gain_copy(t).wait_send()
+    finish_wait(v_fin, v_land, 1)
+    for t in range(rows - 2):
         for h, _, i in parts:
-            gather(*k_ring, t, h, i).wait_send()
-            gather(*v_ring, t, h, i).wait_send()
+            reduce(*dv_ring[2:], t, h, i).wait_send()
             reduce(*dk_ring[2:], t, h, i).wait_send()
-            reduce(*dv_ring[2:], t, h, i).wait_send()
+    finish(*dk_ring, k_fin, k_land, 0)
+
     for j in range(cols - 1):
         for out in outs:
             give(*out, j).wait()
+    for copy in three:
+        copy.wait()
+    for h, _, i in parts:
+        reduce(*dv_ring[2:], rows - 2, h, i).wait_send()
+        reduce(*dk_ring[2:], rows - 2, h, i).wait_send()
     for copy in local:
         copy.wait()
+    finish_wait(k_fin, k_land, 0)
+
+
+def final_kernel(
+    cols, a_ref, dq_ref, dk_ref, dv_ref, g_ref, k_ref, kg_ref, a_out, dq_out, dk_out, dv_out, gq_out, gk_out,
+    a_buf, dq_buf, dk_in, dv_in, g_in, key, kg, dk_buf, dv_buf, gq_buf, gk_buf, sem,
+):
+    _, z, c = place(cols)
+    tok, head = dk_in.shape[1:]
+    ins = [move(src, dst, sem.at[i, 0, 0]) for i, (src, dst) in enumerate(((k_ref, key), (dk_ref, dk_in), (kg_ref, kg), (dv_ref, dv_in), (g_ref, g_in)))]
+    piece = tok // PIECES
+    cuts = [pl.ds(p * piece, piece) for p in range(PIECES)]
+    wide = ((a_ref, a_buf, a_out), (dq_ref, dq_buf, dq_out))
+    come = [move(src.at[p, :], buf.at[p, :], sem.at[9, i, n]) for i, (src, buf, _) in enumerate(wide) for n, p in enumerate(cuts)]
+    big = []
+    for i, (_, buf, dst) in enumerate(wide):
+        for n, p in enumerate(cuts):
+            come[i * PIECES + n].wait()
+            big.append(move(buf.at[p, :], dst.at[p, :], sem.at[10, i, n]))
+    for copy in ins:
+        copy.wait()
+    cut = [slice(i * head, (i + 1) * head) for i in range(cols)]
+    for i in range(cols):
+        raw = key[:, cut[i]].astype(jnp.float32)
+        scale = lax.rsqrt(jnp.mean(raw * raw, -1, keepdims=True) + EPSILON)
+        unit = raw * scale
+        gd = kg[i : i + 1, :] * dk_in[i].astype(jnp.float32)
+        dk_buf[:, cut[i]] = (scale * (gd - unit * jnp.mean(unit * gd, -1, keepdims=True))).astype(jnp.bfloat16)
+        dv_buf[:, cut[i]] = dv_in[i]
+    gq_buf[...] = g_in[z, pl.ds(c, 1), :]
+    gk_buf[...] = jnp.concatenate([g_in[i, cols : cols + 1, :] for i in range(cols)], axis=0)
+    for i, (src, dst) in enumerate(((dk_buf, dk_out), (dv_buf, dv_out), (gq_buf, gq_out), (gk_buf, gk_out))):
+        big.append(move(src, dst, sem.at[5 + i, 0, 0]))
+    for copy in big:
+        copy.wait()
+
+
+def finalize(cols, a, dq, dk, dv, g, keys, k_gain):
+    tok, wide = keys.shape
+    head = wide // cols
+    low, full = jnp.bfloat16, jnp.float32
+    outs = (
+        jax.ShapeDtypeStruct(a.shape, low),
+        jax.ShapeDtypeStruct(dq.shape, low),
+        jax.ShapeDtypeStruct((tok, wide), low),
+        jax.ShapeDtypeStruct((tok, wide), low),
+        jax.ShapeDtypeStruct((1, head), full),
+        jax.ShapeDtypeStruct((cols, head), full),
+    )
+    return pl.pallas_call(
+        functools.partial(final_kernel, cols),
+        out_shape=outs,
+        in_specs=[ANY] * 7,
+        out_specs=(ANY,) * 6,
+        scratch_shapes=[pltpu.VMEM(x.shape, x.dtype) for x in (a, dq, dk, dv, g, keys, k_gain) + outs[2:]]
+        + [pltpu.SemaphoreType.DMA((11, 2, PIECES))],
+        compiler_params=pltpu.CompilerParams(vmem_limit_bytes=LIMIT),
+        cost_estimate=pl.CostEstimate(flops=0, bytes_accessed=8 << 20, transcendentals=0),
+    )(a, dq, dk, dv, g, keys, k_gain)
 
 
 def make_table(rows, cols, per, lists):
     _, z, c = place(cols)
     steps = cols * per
     here = lax.dynamic_slice_in_dim(lists, z * steps, steps, 0)[:, WINDOW + GLOBALS :]
-    turned = lax.dynamic_slice_in_dim(jnp.concatenate([here, here]), per * (c + 1) % steps, steps, 0).reshape(-1)
-    order = jnp.arange(turned.shape[0], dtype=jnp.int32)
-    same = (turned[:, None] == turned[None, :]) & (order[None, :] < order[:, None])
-    prev = jnp.max(jnp.where(same, order[None, :] + 1, 0), axis=1)
+    randoms = here.shape[1]
+    here = here.reshape(-1)
+    place_of = jnp.arange(here.shape[0], dtype=jnp.int32)
+    block, slot = place_of // randoms, place_of % randoms
+    turn = (STRIDE * (block // per - c + cols) - 1) % cols
+    order = (turn * per + block % per) * randoms + slot + 1
+    same = (here[:, None] == here[None, :]) & (order[None, :] < order[:, None])
+    prev = jnp.max(jnp.where(same, order[None, :], 0), axis=1)
     ids = jnp.arange(lists.shape[0], dtype=jnp.int32)
-    last = jnp.max(jnp.where(ids[:, None] == turned[None, :], order[None, :] + 1, 0), axis=1)
-    return jnp.concatenate([turned, prev, last]).astype(jnp.int32)
+    last = jnp.max(jnp.where(ids[:, None] == here[None, :], order[None, :], 0), axis=1)
+    return jnp.concatenate([here, prev, last]).astype(jnp.int32)
 
 
 def on_device(depth, queries, keys, values, grad_out, q_gain, k_gain, block_lists):
@@ -493,18 +580,17 @@
     ring = (rows, 2 * SUBS)
     tile = 2 * heads
     flops = 6 * 2 * group * heads * lists.shape[1] * BLOCK * head
-    a, dq, dk, dv, gain_q, gain_k = pl.pallas_call(
+    a, dq, dk, dv, g = pl.pallas_call(
         functools.partial(kernel, rows, cols, depth, randoms),
         out_shape=(
             jax.ShapeDtypeStruct((tok, wide), low),
             jax.ShapeDtypeStruct((tok, wide), low),
-            jax.ShapeDtypeStruct((tok, head * cols), low),
-            jax.ShapeDtypeStruct((tok, head * cols), low),
-            jax.ShapeDtypeStruct((1, head), full),
-            jax.ShapeDtypeStruct((cols, head), full),
+            jax.ShapeDtypeStruct((cols, tok, head), low),
+            jax.ShapeDtypeStruct((cols, tok, head), low),
+            jax.ShapeDtypeStruct((cols, tile, head), full),
         ),
-        in_specs=[pl.BlockSpec(memory_space=pltpu.SMEM)] + [ANY] * 4 + [VMEM] * 3,
-        out_specs=(ANY, ANY, VMEM, VMEM, VMEM, VMEM),
+        in_specs=[pl.BlockSpec(memory_space=pltpu.SMEM)] + [ANY] * 4 + [VMEM] * 2,
+        out_specs=(ANY,) * 5,
         scratch_shapes=[
             pltpu.VMEM((group, width), low),
             pltpu.VMEM((group, width), low),
@@ -513,7 +599,8 @@
             pltpu.VMEM((rows * steps, BLOCK, head), low),
             pltpu.VMEM((8, head), full),
             pltpu.VMEM((cols, 8, head), full),
-            pltpu.VMEM((rows, cols, head), full),
+            pltpu.VMEM((cols, head), full),
+            pltpu.VMEM((cols, head), full),
             pltpu.VMEM((steps, heads * BLOCK, head), low),
             pltpu.VMEM((steps, heads * BLOCK, lists.shape[1] * BLOCK), low),
             pltpu.VMEM((rows * group, head), full),
@@ -528,12 +615,10 @@
             pltpu.VMEM((rows, group, head), low),
             pltpu.VMEM((group, head), low),
             pltpu.VMEM((group, head), low),
-            pltpu.VMEM((cols, tok, head), low),
-            pltpu.VMEM((cols, tok, head), low),
             pltpu.VMEM((rows, tile, head), full),
             pltpu.VMEM((depth, tile, head), full),
-            pltpu.VMEM((cols, tile, head), full),
-            sem((6,)),
+            pltpu.VMEM((tile, head), full),
+            sem((9,)),
             sem((2, cols)),
             sem((2, cols)),
             sem((2, cols)),
@@ -571,10 +656,10 @@
         grad_out[0],
         keys[0],
         values.reshape(tok // BLOCK, BLOCK, head * cols),
-        keys[0],
         q_gain,
         k_gain,
     )
+    a, dq, dk, dv, gain_q, gain_k = finalize(cols, a, dq, dk, dv, g, keys[0], k_gain)
     return a[None], dq[None], dk[None], dv[None], gain_q, gain_k
 
 

time: 147 us -> 135 us (0.918)
  local copies, waits for them, and re-layouts: 8.05 us -> 0.88 us
  Pallas kernels: 137 us -> 132 us
    pallas_call x1, Pallas kernels: 137 us -> 128 us  [on_device(): pl.pallas_call(functools.partial(kernel, rows, cols, depth, randoms), out...]
    unnamed x18 -> x2, local copies, waits for them, and re-layouts: 7.72 us -> 0.63 us
    pallas_call x0 -> x1, Pallas kernels: none -> 4.24 us  [finalize(): pl.pallas_call(functools.partial(final_kernel, cols), out_shape=outs, in_...]
where the time goes in v3:
time: 135 us
  Pallas kernels  132 us (98%)
    pallas_call x1, Pallas kernels, on_device(): pl.pallas_call(functools.partial(kernel, rows, cols, depth, randoms), out...  128 us
    pallas_call x1, Pallas kernels, finalize(): pl.pallas_call(functools.partial(final_kernel, cols), out_shape=outs, in_...  4.24 us

profile of v3, /device:TPU:1, one launch (start us, length us, event | category | flops | bytes accessed | tf_op | source)
XLA Modules:
  0.0 134.9 jit_solution(18403249101349125960)
XLA Ops:
  0.6 0.0 copy-start
  0.7 0.6 copy-done
  1.3 0.1 dynamic-slice_bitcast_fusion
  1.4 0.1 copy.15
  1.5 0.1 reshape.147
  1.6 0.1 select_reduce_fusion
  1.7 0.2 select_reduce_fusion.1
  1.9 0.6 pad_add_fusion.table
  2.5 128.2 %shard_map.118 = (bf16[128,8192]{1,0:T(8,128)(2,1)}, bf16[128,8192]{1,0:T(8,128)(2,1)}, bf16[8,128,128]{2,1,0:T(8,128)(2,1)}, bf16[8,128,128]{2,1,0:T(8,128)(2,1)}, f32[8,16,128]{2,1,0:T(8,128)}) custom-call(s32[224]{0:T(256)} %pad_add_fusion.table, bf16[128,8192]{1,0:T(8,128)(2,1)} %bitcast.12, bf16[128,8192]{1,0:T(8,128)(2,1)} %bitcast.13, ...), custom_call_target="tpu_custom_call" | custom-call | flops 6442450944 | bytes 16777216 | tf_op jit(solution)/shard_map/pallas_call | solution.py:583
  130.7 4.2 %shard_map.119 = (bf16[128,8192]{1,0:T(8,128)(2,1)}, bf16[128,8192]{1,0:T(8,128)(2,1)}, bf16[128,1024]{1,0:T(8,128)(2,1)}, bf16[128,1024]{1,0:T(8,128)(2,1)}, f32[1,128]{1,0:T(1,128)}, /*index=5*/f32[8,128]{1,0:T(8,128)}) custom-call(bf16[128,8192]{1,0:T(8,128)(2,1)} %get-tuple-element.17.a_ref, bf16[128,8192]{1,0:T(8,128)(2,1)} %get-tuple-element.18.dq_ref, ...), custom_call_target="tpu_custom_call" | custom-call | bytes 8388608 | tf_op jit(solution)/shard_map/pallas_call | solution.py:537
  (2 shorter events, 0.0 us)
Async XLA Ops:
  0.6 0.7 copy-start

commit v4 on v3

--- a/solution.py
+++ b/solution.py
@@ -10,13 +10,13 @@
 
 EPSILON = 1e-06
 BLOCK = 64
-SUBS = 2
+SUBS = 1
 MESH = pl.DeviceIdType.MESH
 ANY = pl.BlockSpec(memory_space=pl.ANY)
 VMEM = pl.BlockSpec(memory_space=pltpu.VMEM)
 LIMIT = 60 * 1024 * 1024
 WINDOW, GLOBALS = 3, 2
-LAG, GO_FROM, STRIDE = 2, 3, 3
+GO_AT, STRIDE = (0, 3, 7, 7, 7), 5
 PIECES = 2
 
 
@@ -97,6 +97,7 @@
     dv_rand,
     gq_acc,
     gk_acc,
+    delta,
     ax,
     dqx,
     k_sum,
@@ -157,7 +158,8 @@
     right, left = along[1], along[rows - 1]
     mine = aligned(c, tok)
     mine_wide = aligned(c, width)
-    parts = [(h, s, h * SUBS + s) for s in range(SUBS) for h in range(2)]
+    hops = rows // 2
+    parts = [(dr, h, h * SUBS + s) for s in range(SUBS) for h in range(2) for dr in range(2)]
 
     gain[...] = jnp.broadcast_to(qg_ref[...], gain.shape)
     greet(list(across.values()) + list(along.values()) + list(over.values()))
@@ -177,14 +179,16 @@
 
     def bring(i, src, dst, d):
         part = aligned(lax.rem(c + d, cols), width)
-        return push(src.at[:, part], dst.at[mine, :], in_send.at[i, d], in_recv.at[i, d], across[d])
+        return wire(src.at[:, part], dst.at[mine, :], in_send.at[i, d], in_recv.at[i, d], at(z, c + d))
 
     q_in = [bring(0, q_ref, qx, d) for d in range(1, cols)]
+    for copy in q_in:
+        copy.start()
     own_q = move(q_ref.at[:, mine_wide], qx.at[mine, :], own_sem.at[2])
     own_go = move(go_ref.at[:, mine_wide], gox.at[mine, :], own_sem.at[3])
     for ref in (dk_base, dv_base, gq_acc, gk_acc):
         ref[...] = jnp.zeros_like(ref)
-    for ref in (dk_rand, dv_rand, k_sum, v_sum):
+    for ref in (dk_rand, dv_rand):
         ref[0] = jnp.zeros(ref.shape[1:], ref.dtype)
 
     own_k.wait()
@@ -205,35 +209,43 @@
         gq_own[...] = gz[...]
 
 
-    def gather(ref, send, recv, t, h, i):
-        slot = lax.rem(z + t, rows) if h else lax.rem(z + rows - t, rows)
+    def gather(ref, send, recv, t, dr, i):
+        slot = lax.rem(z + t, rows) if dr else lax.rem(z + rows - t, rows)
         part = pl.ds(slot * steps + i * (sub // BLOCK), sub // BLOCK)
-        return wire(ref.at[part], ref.at[part], send.at[t, i], recv.at[t, i], left if h else right)
-
-    def gather_step(ref, send, recv, t, waits=True):
-        for h, _, i in parts:
-            if waits:
-                gather(ref, send, recv, t - 1, h, i).wait_recv()
-            gather(ref, send, recv, t, h, i).start()
+        m = dr * 2 * SUBS + i
+        return wire(ref.at[part], ref.at[part], send.at[t, m], recv.at[t, m], left if dr else right)
+
+    def gather_parts(t):
+        return [(dr, i) for dr, h, i in parts if t < hops - 1 or h == dr]
+
+    def gather_step(ref, send, recv, t):
+        for dr, i in gather_parts(t):
+            if t:
+                gather(ref, send, recv, t - 1, dr, i).wait_recv()
+            gather(ref, send, recv, t, dr, i).start()
+
+    def gather_end(ref, send, recv):
+        last = gather_parts(hops - 1)
+        for dr, i in gather_parts(hops - 2):
+            if (dr, i) not in last:
+                gather(ref, send, recv, hops - 2, dr, i).wait_recv()
+        for dr, i in last:
+            gather(ref, send, recv, hops - 1, dr, i).wait_recv()
 
     k_ring, v_ring = (kall, k_send, k_recv), (vall, v_send, v_recv)
-
-    lag, lag_out, go_from = LAG, rows // 2, GO_FROM
-    go_in = []
-    for t in range(rows - 1):
-        gather_step(*k_ring, t, t > 0)
-        if t >= lag:
-            if t == lag:
-                own_v.wait()
-                for copy in late:
-                    copy.wait()
-            gather_step(*v_ring, t - lag, t > lag)
-        if t >= go_from:
-            more = -(-(cols - 1) // (rows - 1 - go_from))
-            for d in [-STRIDE * (j + 1) % cols for j in range(cols - 1)][(t - go_from) * more : (t - go_from + 1) * more]:
-                go_in.append(bring(1, go_ref, gox, d))
-    for h, _, i in parts:
-        gather(*k_ring, rows - 2, h, i).wait_recv()
+    order = [-STRIDE * (j + 1) % cols for j in range(cols - 1)]
+    go_in = [bring(1, go_ref, gox, d) for d in order]
+    for t in range(hops):
+        gather_step(*k_ring, t)
+        if t == 1:
+            own_v.wait()
+            for copy in late:
+                copy.wait()
+        if t:
+            gather_step(*v_ring, t - 1)
+        for copy in go_in[GO_AT[t] : GO_AT[t + 1]]:
+            copy.start()
+    gather_end(*k_ring)
 
     @pl.when(z != c)
     def _():
@@ -283,81 +295,92 @@
         expo = jnp.exp2(scores * (score_scale * math.log2(math.e)))
         probs[n] = (expo * (1.0 / jnp.sum(expo, axis=1, keepdims=True))).astype(low)
 
-    def make_dv(i):
+    def make_out(i):
         n = block_of(i)
-        spread(dv_base, dv_rand, i, n, dot(probs[n], cotangents(n), ((0,), (0,))))
-
-    def make_rest(i):
+        prob, grad = probs[n], cotangents(n)
+        out = dot(prob, listed(vall, n), ((1,), (0,)))
+        delta[n] = jnp.sum(out * grad.astype(jnp.float32), axis=1, keepdims=True)
+        for h in range(heads):
+            ax[aligned(n, BLOCK), cut[h]] = out[h * BLOCK : (h + 1) * BLOCK].astype(low)
+        spread(dv_base, dv_rand, i, n, dot(prob, grad, ((0,), (0,))))
+
+    def make_dk(i):
         n = block_of(i)
-        key, value, grad, prob = listed(kall, n), listed(vall, n), cotangents(n), probs[n]
-        out = dot(prob, value, ((1,), (0,)))
-        dprobs = dot(grad, value, ((1,), (1,)))
-        delta = jnp.sum(out * grad.astype(jnp.float32), axis=1, keepdims=True)
-        dscores = (prob.astype(jnp.float32) * (dprobs - delta)).astype(low)
-        dq = dot(dscores, key, ((1,), (0,))) * score_scale
+        key = listed(kall, n)
+        dprobs = dot(cotangents(n), listed(vall, n), ((1,), (1,)))
+        dscores = (probs[n].astype(jnp.float32) * (dprobs - delta[n])).astype(low)
         dk = dot(dscores, qn[n], ((0,), (0,))) * score_scale
         spread(dk_base, dk_rand, i, n, dk)
         gk_acc[...] += jnp.sum(dk * key.astype(jnp.float32), axis=0, keepdims=True)
+        probs[n] = dscores
+
+    def make_dq(i):
+        n = block_of(i)
+        dq = dot(probs[n], listed(kall, n), ((1,), (0,))) * score_scale
         units, scales = unit_queries(n)
         for h in range(heads):
-            part = slice(h * BLOCK, (h + 1) * BLOCK)
-            ax[aligned(n, BLOCK), cut[h]] = out[part].astype(low)
-            d, unit = dq[part], units[h]
+            d, unit = dq[h * BLOCK : (h + 1) * BLOCK], units[h]
             gq_acc[h : h + 1, :] += jnp.sum(d * unit, 0, keepdims=True)
             gd = gains[h] * d
             dqx[aligned(n, BLOCK), cut[h]] = (
                 scales[h] * (gd - unit * jnp.mean(unit * gd, -1, keepdims=True))
             ).astype(low)
 
-    def pair(work, j):
+    def pair(make, j):
         for p in range(per):
-            work(j * per + p)
-
-    early = rows - 1 - lag
-    share = cols // lag if lag else cols
-
-    def probs_pair(j):
+            make(j * per + p)
+
+    def probs_step(j, _):
         pair(make_probs, j)
         return 0
 
-    def probs_step(u, _):
-        gather_step(*v_ring, u + early)
-        lax.fori_loop(0, share, lambda w, _: probs_pair(u * share + w), 0)
-        return 0
-
-    if lag:
-        lax.fori_loop(0, lag, probs_step, 0)
-    else:
-        for w in range(cols):
-            pair(make_probs, w)
-
+    lax.fori_loop(0, cols // 2, probs_step, 0)
+    gather_step(*v_ring, hops - 1)
+    lax.fori_loop(cols // 2, cols, probs_step, 0)
 
     @pl.when(z == c)
     def _():
         for copy in served:
             copy.wait_send()
 
-    for t in range(rows - 2):
-        for h, _, i in parts:
-            gather(*k_ring, t, h, i).wait_send()
-            gather(*v_ring, t, h, i).wait_send()
+    for t in range(hops):
+        for dr, i in gather_parts(t):
+            gather(*k_ring, t, dr, i).wait_send()
     own_go.wait()
-    for copy in go_in:
-        copy.wait()
-
-    def dv_step(j, _):
-        pair(make_dv, j)
+
+    gather_end(*v_ring)
+
+    def give(i, src, dst, j):
+        part = aligned(owner(j), tok)
+        to = at(z, owner(j))
+        return wire(src.at[part, :], dst.at[:, mine_wide], out_send.at[i, j], out_recv.at[i, j], to)
+
+    outs = ((0, ax, a_out), (1, dqx, dq_out))
+
+    def out_step(j, _):
+        @pl.when(j < cols - 1)
+        def _():
+            bring(1, go_ref, gox, lax.rem((cols - STRIDE) * (j + 1), cols)).wait_recv()
+
+        pair(make_out, j)
+
+        @pl.when(j < cols - 1)
+        def _():
+            give(*outs[0], j).start()
+
         return 0
 
-    lax.fori_loop(0, cols, dv_step, 0)
-    for h, _, i in parts:
-        gather(*v_ring, rows - 2, h, i).wait_recv()
-        gather(*k_ring, rows - 2, h, i).wait_send()
-        gather(*v_ring, rows - 2, h, i).wait_send()
-
-    def reduce(sums, send, recv, t, h, i):
+    lax.fori_loop(0, cols, out_step, 0)
+
+    def reduce(sums, send, recv, t, dr, i):
         part = pl.ds(i * sub, sub)
-        return wire(sums.at[t, part, :], sums.at[t + 1, part, :], send.at[t, i], recv.at[t, i], left if h else right)
+        m = dr * 2 * SUBS + i
+        return wire(
+            sums.at[dr, t, part, :], sums.at[dr, t + 1, part, :], send.at[t, m], recv.at[t, m], left if dr else right
+        )
+
+    def reduce_parts(t):
+        return [(dr, i) for dr, h, i in parts if t or h == dr]
 
     def own_part(base, rand, chunk, i):
         start = chunk * group + i * sub
@@ -370,28 +393,30 @@
             axis=0,
         )
 
-    def reduce_step(base, rand, sums, send, recv, t, waits):
-        for h, _, i in parts:
-            chunk = lax.rem(z + 1 + t, rows) if h else lax.rem(z + 2 * rows - 1 - t, rows)
-            own = own_part(base, rand, chunk, i)
-            if waits is True:
-                reduce(sums, send, recv, t - 1, h, i).wait_recv()
-            elif waits is not False:
-
-                @pl.when(waits)
-                def _():
-                    reduce(sums, send, recv, t - 1, h, i).wait_recv()
-
+    def reduce_step(base, rand, sums, send, recv, t):
+        for dr, i in reduce_parts(t):
+            far = hops - t
+            chunk = lax.rem(z + rows - far, rows) if dr else lax.rem(z + far, rows)
+            total = own_part(base, rand, chunk, i)
             part = pl.ds(i * sub, sub)
-            sums[t, part, :] = (sums[t, part, :].astype(jnp.float32) + own).astype(low)
-            reduce(sums, send, recv, t, h, i).start()
+            if t and (dr, i) in reduce_parts(t - 1):
+                reduce(sums, send, recv, t - 1, dr, i).wait_recv()
+                total += sums[dr, t, part, :].astype(jnp.float32)
+            sums[dr, t, part, :] = total.astype(low)
+            reduce(sums, send, recv, t, dr, i).start()
+
+    def reduce_sent(sums, send, recv, t):
+        for dr, i in reduce_parts(t):
+            reduce(sums, send, recv, t, dr, i).wait_send()
 
     def finish(base, rand, sums, send, recv, fin, land, w):
-        for h, _, i in parts:
-            own = own_part(base, rand, z, i)
-            reduce(sums, send, recv, rows - 2, h, i).wait_recv()
+        for i in [i for dr, _, i in parts if dr]:
             part = pl.ds(i * sub, sub)
-            fin[part, :] = (sums[rows - 1, part, :].astype(jnp.float32) + own).astype(low)
+            total = own_part(base, rand, z, i)
+            for dr in range(2):
+                reduce(sums, send, recv, hops - 1, dr, i).wait_recv()
+                total += sums[dr, hops, part, :].astype(jnp.float32)
+            fin[part, :] = total.astype(low)
             for cc in range(i * sub // tok, (i + 1) * sub // tok):
                 d = lax.rem(cc - c + cols, cols)
 
@@ -411,68 +436,64 @@
     dk_ring = (dk_base, dk_rand, k_sum, dk_send, dk_recv)
     dv_ring = (dv_base, dv_rand, v_sum, dv_send, dv_recv)
 
-    def give(i, src, dst, j):
-        part = aligned(owner(j), tok)
-        to = at(z, owner(j))
-        return wire(src.at[part, :], dst.at[:, mine_wide], out_send.at[i, j], out_recv.at[i, j], to)
-
-    outs = ((0, ax, a_out), (1, dqx, dq_out))
-
-    early = rows - 1 - lag_out
-    share = cols // lag_out
-
-    def rest_step(u, _):
-        reduce_step(*dv_ring, u, u > 0)
-        for w in range(share):
-            j = u * share + w
-            pair(make_rest, j)
+    def dk_work(start, stop):
+        def step(j, _):
+            pair(make_dk, j)
+            return 0
+
+        lax.fori_loop(start, stop, step, 0)
+
+    def dq_work(start, stop):
+        def step(j, _):
+            pair(make_dq, j)
 
             @pl.when(j < cols - 1)
             def _():
-                for out in outs:
-                    give(*out, j).start()
-
-        return 0
-
-    lax.fori_loop(0, lag_out, rest_step, 0)
+                give(*outs[1], j).start()
+
+            return 0
+
+        lax.fori_loop(start, stop, step, 0)
+
+    half = cols // 2
+    reduce_step(*dv_ring, 0)
+    dk_work(0, half)
+    reduce_step(*dv_ring, 1)
+    dk_work(half, cols)
+    reduce_step(*dk_ring, 0)
+    for t in range(hops):
+        for dr, i in gather_parts(t):
+            gather(*v_ring, t, dr, i).wait_send()
+    reduce_step(*dv_ring, 2)
+    dq_work(0, half)
+    reduce_step(*dk_ring, 1)
+    reduce_step(*dv_ring, 3)
+    dq_work(half, cols)
     for i, src, dst in outs:
         local.append(move(src.at[mine, :], dst.at[:, mine_wide], own_sem.at[4 + i]))
     gp = g1.at[z]
     gp[:heads, :] = gq_acc[...]
     gp[heads:, :] = jnp.broadcast_to(gk_acc[...] / kg_ref[pl.ds(c, 1), :], (heads, head))
-
-    reduce_step(*dk_ring, 0, False)
     one = [push(gp, gp, g1_send.at[d], g1_recv.at[d], along[d]) for d in range(1, rows)]
-    reduce_step(*dv_ring, lag_out, True)
-
-    def both_step(u, _):
-        reduce_step(*dk_ring, u, True)
-        reduce_step(*dv_ring, u + lag_out, True)
-        return 0
-
-    lax.fori_loop(1, early, both_step, 0)
+    reduce_step(*dk_ring, 2)
     for copy in one:
         copy.wait()
     g2[dp] = jnp.sum(g1[...], 0)
     two = [push(g2.at[dp], g2.at[dp], g2_send.at[d], g2_recv.at[d], over[d]) for d in range(1, depth)]
     finish(*dv_ring, v_fin, v_land, 1)
-
-    def dk_step(u, _):
-        reduce_step(*dk_ring, u, True)
-        return 0
-
-    lax.fori_loop(early, rows - 2, dk_step, 0)
+    for t in range(hops):
+        reduce_sent(*dv_ring[2:], t)
+    for copy in go_in:
+        copy.wait_send()
+    reduce_step(*dk_ring, 3)
     for copy in two:
         copy.wait()
     g2_sum[...] = jnp.sum(g2[...], 0)
     three = [push(g2_sum, g3.at[c], g3_send.at[d], g3_recv.at[d], across[d]) for d in range(1, cols)]
     local.append(move(g2_sum, g3.at[c], own_sem.at[8]))
-    reduce_step(*dk_ring, rows - 2, True)
     finish_wait(v_fin, v_land, 1)
-    for t in range(rows - 2):
-        for h, _, i in parts:
-            reduce(*dv_ring[2:], t, h, i).wait_send()
-            reduce(*dk_ring[2:], t, h, i).wait_send()
+    for t in range(hops - 1):
+        reduce_sent(*dk_ring[2:], t)
     finish(*dk_ring, k_fin, k_land, 0)
 
     for j in range(cols - 1):
@@ -480,9 +501,7 @@
             give(*out, j).wait()
     for copy in three:
         copy.wait()
-    for h, _, i in parts:
-        reduce(*dv_ring[2:], rows - 2, h, i).wait_send()
-        reduce(*dk_ring[2:], rows - 2, h, i).wait_send()
+    reduce_sent(*dk_ring[2:], hops - 1)
     for copy in local:
         copy.wait()
     finish_wait(k_fin, k_land, 0)
@@ -577,7 +596,7 @@
     table = make_table(rows, cols, tok // BLOCK, lists)
     low, full = jnp.bfloat16, jnp.float32
     sem = pltpu.SemaphoreType.DMA
-    ring = (rows, 2 * SUBS)
+    ring = (rows // 2, 4 * SUBS)
     tile = 2 * heads
     flops = 6 * 2 * group * heads * lists.shape[1] * BLOCK * head
     a, dq, dk, dv, g = pl.pallas_call(
@@ -609,10 +628,11 @@
             pltpu.VMEM((steps * randoms + 1, BLOCK, head), full),
             pltpu.VMEM((heads, head), full),
             pltpu.VMEM((1, head), full),
+            pltpu.VMEM((steps, heads * BLOCK, 1), full),
             pltpu.VMEM((group, width), low),
             pltpu.VMEM((group, width), low),
-            pltpu.VMEM((rows, group, head), low),
-            pltpu.VMEM((rows, group, head), low),
+            pltpu.VMEM((2, rows // 2 + 1, group, head), low),
+            pltpu.VMEM((2, rows // 2 + 1, group, head), low),
             pltpu.VMEM((group, head), low),
             pltpu.VMEM((group, head), low),
             pltpu.VMEM((rows, tile, head), full),

time: 135 us -> 127 us (0.941)
  Pallas kernels: 132 us -> 124 us
    pallas_call x1, Pallas kernels: 128 us -> 120 us  [on_device(): pl.pallas_call(functools.partial(kernel, rows, cols, depth, randoms), out...]
where the time goes in v4:
time: 127 us
  Pallas kernels  124 us (98%)
    pallas_call x1, Pallas kernels, on_device(): pl.pallas_call(functools.partial(kernel, rows, cols, depth, randoms), out...  120 us
    pallas_call x1, Pallas kernels, finalize(): pl.pallas_call(functools.partial(final_kernel, cols), out_shape=outs, in_...  4.24 us

profile of v4, /device:TPU:1, one launch (start us, length us, event | category | flops | bytes accessed | tf_op | source)
XLA Modules:
  0.0 126.8 jit_solution(3374904503054935658)
XLA Ops:
  0.6 0.0 copy-start
  0.7 0.6 copy-done
  1.3 0.1 dynamic-slice_bitcast_fusion
  1.4 0.1 copy.15
  1.5 0.1 reshape.147
  1.6 0.1 select_reduce_fusion
  1.7 0.2 select_reduce_fusion.1
  1.9 0.6 pad_add_fusion.table
  2.5 120.0 %shard_map.118 = (bf16[128,8192]{1,0:T(8,128)(2,1)}, bf16[128,8192]{1,0:T(8,128)(2,1)}, bf16[8,128,128]{2,1,0:T(8,128)(2,1)}, bf16[8,128,128]{2,1,0:T(8,128)(2,1)}, f32[8,16,128]{2,1,0:T(8,128)}) custom-call(s32[224]{0:T(256)} %pad_add_fusion.table, bf16[128,8192]{1,0:T(8,128)(2,1)} %bitcast.12, bf16[128,8192]{1,0:T(8,128)(2,1)} %bitcast.13, ...), custom_call_target="tpu_custom_call" | custom-call | flops 6442450944 | bytes 16777216 | tf_op jit(solution)/shard_map/pallas_call | solution.py:602
  122.5 4.2 %shard_map.119 = (bf16[128,8192]{1,0:T(8,128)(2,1)}, bf16[128,8192]{1,0:T(8,128)(2,1)}, bf16[128,1024]{1,0:T(8,128)(2,1)}, bf16[128,1024]{1,0:T(8,128)(2,1)}, f32[1,128]{1,0:T(1,128)}, /*index=5*/f32[8,128]{1,0:T(8,128)}) custom-call(bf16[128,8192]{1,0:T(8,128)(2,1)} %get-tuple-element.17.a_ref, bf16[128,8192]{1,0:T(8,128)(2,1)} %get-tuple-element.18.dq_ref, ...), custom_call_target="tpu_custom_call" | custom-call | bytes 8388608 | tf_op jit(solution)/shard_map/pallas_call | solution.py:556
  (2 shorter events, 0.0 us)
Async XLA Ops:
  0.6 0.7 copy-start
